TPU v7x, 512 devices: a whole 4x8x8 slice. The times are simulated.
512 devices in a mesh: nodes: 64 (over z, x, y_lo), feat: 8 (over y_hi, core).
Axes of the slice: x: 4, y: 8 (y_hi: 4, y_lo: 2; y = y_hi * 2 + y_lo), z: 8, core: 2. Of those that a mesh axis runs over, the one named last changes fastest.
Arguments:
- features: bfloat16 [65536, 768], P('nodes', 'feat'), may hold values from -6 to 6
- target_ids: int32 [16384], P('nodes'), may hold values from 0 to 1023
- near_ids: int32 [16384, 25], P('nodes'), may hold values from 0 to 1023
- seed_ids: int32 [16384], P('nodes'), may hold values from 0 to 255
- seed_near: int32 [16384, 15], P('nodes'), may hold values from 0 to 255
- w1_self: bfloat16 [768, 1024], P('feat'), may hold values from -0.21875 to 0.21875
- w1_neigh: bfloat16 [768, 1024], P('feat'), may hold values from -0.21875 to 0.21875
- w2_self: bfloat16 [1024, 153], P('feat'), may hold values from -0.1875 to 0.1875
- w2_neigh: bfloat16 [1024, 153], P('feat'), may hold values from -0.1875 to 0.1875
- logit_grad: bfloat16 [16384, 153], P('nodes'), may hold values from -6 to 6
Outputs:
- logits: float32 [16384, 153], P('nodes')
- grad_w1_self: float32 [768, 1024], P('feat')
- grad_w1_neigh: float32 [768, 1024], P('feat')
- grad_w2_self: float32 [1024, 153], P('feat')
- grad_w2_neigh: float32 [1024, 153], P('feat')
All inputs are finite; a program needn't handle non-finite values.
Results may differ from a plain program's by a relative error of at most 0.025.
Values may be sent and summed in bfloat16 or wider, within the bound.
A program may use at most 64 MiB of HBM per device.

v0:
```python
import jax
import jax.numpy as jnp
from jax import lax
from jax.sharding import PartitionSpec as P


def local(
    features,
    target_ids,
    near_ids,
    seed_ids,
    seed_near,
    w1_self,
    w1_neigh,
    w2_self,
    w2_neigh,
    logit_grad,
):
    row_count = target_ids.shape[0]
    fan_one = near_ids.shape[1]
    fan_two = seed_near.shape[1]
    x_self = features[target_ids]

    def add_neighbour(column, running):
        neighbour_rows = lax.dynamic_index_in_dim(near_ids, column, 1, keepdims=False)
        return running + features[neighbour_rows].astype(jnp.float32)

    running = lax.fori_loop(
        0, fan_one, add_neighbour, jnp.zeros((row_count, features.shape[1]), jnp.float32)
    )
    agg_one = (running / fan_one).astype(jnp.bfloat16)
    share_width = w1_self.shape[1] // lax.axis_size("feat")
    weight_rows = (((0,), (1,)), ((), ()))
    result = lax.dot_general(w1_self, x_self, weight_rows, preferred_element_type=jnp.float32)
    summed_all = lax.psum(
        (
            result
            + lax.dot_general(w1_neigh, agg_one, weight_rows, preferred_element_type=jnp.float32)
        ).astype(jnp.bfloat16),
        "feat",
    ).astype(jnp.float32)
    pre_share = lax.dynamic_slice_in_dim(
        summed_all, lax.axis_index("feat") * share_width, share_width, 0
    )
    sigma = 1.0 / (1.0 + jnp.exp(-pre_share))
    hidden = (pre_share * sigma).astype(jnp.bfloat16)
    received = lax.all_to_all(hidden, "nodes", split_axis=1, concat_axis=1, tiled=True)
    positions = lax.iota(jnp.int32, received.shape[1])
    selector = (seed_ids[:, None] == positions[None, :]).astype(jnp.bfloat16)
    tallies = jnp.zeros((seed_ids.shape[0], received.shape[1]), jnp.float32)
    for column in range(fan_two):
        tallies = tallies + (seed_near[:, column][:, None] == positions[None, :]).astype(
            jnp.float32
        )
    tallies = tallies.astype(jnp.bfloat16)
    last_dims = (((1,), (1,)), ((), ()))
    first_dims = (((0,), (0,)), ((), ()))
    h_self = lax.dot_general(
        selector, received, last_dims, preferred_element_type=jnp.float32
    ).astype(jnp.bfloat16)
    agg_two = (
        lax.dot_general(tallies, received, last_dims, preferred_element_type=jnp.float32) / fan_two
    ).astype(jnp.bfloat16)
    logit_part = jnp.dot(h_self, w2_self, preferred_element_type=jnp.float32) + jnp.dot(
        agg_two, w2_neigh, preferred_element_type=jnp.float32
    )
    logits = lax.psum(logit_part.astype(jnp.bfloat16), "feat").astype(jnp.float32)
    upper_terms = jnp.stack(
        [
            lax.dot_general(h_self, logit_grad, first_dims, preferred_element_type=jnp.float32),
            lax.dot_general(agg_two, logit_grad, first_dims, preferred_element_type=jnp.float32),
        ]
    )
    g_self = lax.dot_general(
        logit_grad, w2_self, last_dims, preferred_element_type=jnp.float32
    ).astype(jnp.bfloat16)
    g_neigh = lax.dot_general(
        logit_grad, w2_neigh, last_dims, preferred_element_type=jnp.float32
    ).astype(jnp.bfloat16)
    d_received = lax.dot_general(g_self, selector, first_dims, preferred_element_type=jnp.float32)
    d_received = (
        d_received
        + lax.dot_general(g_neigh, tallies, first_dims, preferred_element_type=jnp.float32)
        / fan_two
    )
    d_hidden = lax.all_to_all(
        d_received.astype(jnp.bfloat16), "nodes", split_axis=1, concat_axis=1, tiled=True
    )
    slope = sigma * (1.0 + pre_share * (1.0 - sigma))
    d_pre = (d_hidden.astype(jnp.float32) * slope).astype(jnp.bfloat16)
    shard_piece = lax.all_gather(d_pre, "feat", axis=0, tiled=True)
    lower_grads = jnp.stack(
        [
            lax.dot_general(x_self, shard_piece, weight_rows, preferred_element_type=jnp.float32),
            lax.dot_general(agg_one, shard_piece, weight_rows, preferred_element_type=jnp.float32),
        ]
    )
    lower_grads, upper_terms = lax.psum((lower_grads, upper_terms), "nodes")
    return (logits, lower_grads[0], lower_grads[1], upper_terms[0], upper_terms[1])


def solution(mesh):
    return jax.shard_map(
        local,
        mesh=mesh,
        in_specs=(
            P("nodes", "feat"),
            P("nodes"),
            P("nodes", None),
            P("nodes"),
            P("nodes", None),
            P("feat", None),
            P("feat", None),
            P("feat", None),
            P("feat", None),
            P("nodes", None),
        ),
        out_specs=(
            P("nodes", None),
            P("feat", None),
            P("feat", None),
            P("feat", None),
            P("feat", None),
        ),
        check_vma=False,
    )
```

profile of v0, /device:TPU:2, one launch (start us, length us, event | category | flops | bytes accessed | tf_op | source)
XLA Modules:
  0.0 861.6 jit_solution(69507928125559454)
XLA Ops:
  7.2 1.1 copy.18
  8.4 0.9 gather_fusion.1
  9.3 40.6 %while.14 = (s32[]{:T(128)}, f32[256,96]{1,0:T(8,128)S(1)}, s32[256,25]{0,1:T(8,128)}, bf16[1024,96]{1,0:T(8,128)(2,1)S(1)}, s32[]{:T(128)}, /*index=5*/s32[]{:T(128)}) while((s32[]{:T(128)}, f32[256,96]{1,0:T(8,128)S(1)}, s32[256,25]{0,1:T(8,128)}, bf16[1024,96]{1,0:T(8,128)(2,1)S(1)}, s32[]{:T(128)}, /*index=5*/s32[]{:T(128)}) %tuple.55), condition=%wide.region_1.2_spmd.clone, body=%wide.region_0.1_spmd.clone.sunk | while | flops 75523 | bytes 352339 | solution.py:28
  9.3 0.7 compare_select_fusion.3
  10.0 0.9 gather_fusion
  10.9 0.7 compare_select_fusion.3
  11.6 0.9 gather_fusion
  12.5 0.7 compare_select_fusion.3
  13.2 0.9 gather_fusion
  14.2 0.7 compare_select_fusion.3
  14.9 0.9 gather_fusion
  15.8 0.7 compare_select_fusion.3
  16.5 0.9 gather_fusion
  17.4 0.7 compare_select_fusion.3
  18.1 0.9 gather_fusion
  19.0 0.7 compare_select_fusion.3
  19.8 0.9 gather_fusion
  20.7 0.7 compare_select_fusion.3
  21.4 0.9 gather_fusion
  22.3 0.7 compare_select_fusion.3
  23.0 0.9 gather_fusion
  23.9 0.7 compare_select_fusion.3
  24.6 0.9 gather_fusion
  25.5 0.7 compare_select_fusion.3
  26.3 0.9 gather_fusion
  27.2 0.7 compare_select_fusion.3
  27.9 0.9 gather_fusion
  28.8 0.7 compare_select_fusion.3
  29.5 0.9 gather_fusion
  30.4 0.7 compare_select_fusion.3
  31.1 0.9 gather_fusion
  32.0 0.7 compare_select_fusion.3
  32.8 0.9 gather_fusion
  33.7 0.7 compare_select_fusion.3
  34.4 0.9 gather_fusion
  35.3 0.7 compare_select_fusion.3
  36.0 0.9 gather_fusion
  36.9 0.7 compare_select_fusion.3
  37.6 0.9 gather_fusion
  39.3 0.9 gather_fusion
  40.9 0.9 gather_fusion
  42.5 0.9 gather_fusion
  44.1 0.9 gather_fusion
  45.8 0.9 gather_fusion
  47.4 0.9 gather_fusion
  49.0 0.9 gather_fusion
  50.9 1.1 fusion.1
  52.7 0.8 copy-done.1
  53.5 1.0 convolution_multiply_fusion
  55.0 0.7 copy.20
  55.7 14.9 %all-to-all-start.1 = ((bf16[128,64,4]{0,2,1:T(4,128)(2,1)}), bf16[128,64,4]{0,2,1:T(4,128)(2,1)S(1)}, u32[]{:S(2)}, u32[]{:S(2)}) async-start(bf16[128,64,4]{0,2,1:T(4,128)(2,1)} %bitcast.18), calls=%async_computation.1 | async-start | bytes 131072 | tf_op jit(solution)/shard_map/all_to_all | solution.py:86
  70.6 9.6 %all-to-all-done.1 = bf16[128,64,4]{0,2,1:T(4,128)(2,1)S(1)} async-done(((bf16[128,64,4]{0,2,1:T(4,128)(2,1)}), bf16[128,64,4]{0,2,1:T(4,128)(2,1)S(1)}, u32[]{:S(2)}, u32[]{:S(2)}) %all-to-all-start.1) | async-done | bytes 65568 | tf_op jit(solution)/shard_map/all_to_all | solution.py:86
  80.2 55.7 %all-reduce.5.cloned.1.call-done = bf16[1024,256]{0,1:T(8,128)(2,1)} async-done(((bf16[1024,256]{0,1:T(8,128)(2,1)}), bf16[1024,256]{0,1:T(8,128)(2,1)}) %all-reduce.5.cloned.1.call-update) | async-done | bytes 524304 | tf_op jit(solution)/shard_map/psum | solution.py:35
  135.9 1.5 fusion.8
  137.4 15.3 %all_gather.3 = bf16[1024,256]{0,1:T(8,128)(2,1)S(1)} all-gather(bf16[128,256]{0,1:T(8,128)(2,1)S(1)} %get-tuple-element.120), channel_id=1, replica_groups=mesh['nodes'=64,'feat'=8] {'feat'}, dimensions={0}, use_global_device_ids=true | all-gather | bytes 589824 | tf_op jit(solution)/shard_map/all_gather | solution.py:91
  153.3 12.1 %all-to-all-start = ((bf16[128,64,4]{0,2,1:T(4,128)(2,1)}), bf16[128,64,4]{0,2,1:T(4,128)(2,1)S(1)}, u32[]{:S(2)}, u32[]{:S(2)}) async-start(bf16[128,64,4]{0,2,1:T(4,128)(2,1)} %bitcast.1), calls=%async_computation | async-start | bytes 131072 | tf_op jit(solution)/shard_map/all_to_all | solution.py:47
  165.4 0.9 pad_maximum_fusion
  166.3 8.5 all-to-all-done
  174.9 1.0 fusion.3
  176.6 0.8 fusion.2
  178.2 64.2 %all-reduce.7.cloned.1.call-done = bf16[256,153]{0,1:T(8,128)(2,1)} async-done(((bf16[256,153]{0,1:T(8,128)(2,1)}), bf16[256,153]{0,1:T(8,128)(2,1)}) %all-reduce.7.cloned.1.call-update) | async-done | bytes 78352 | tf_op jit(solution)/shard_map/psum | solution.py:67
  242.4 1.6 convert_element_type.125
  244.0 608.3 %all-reduce.9.cloned.1.call-done = (f32[2,96,1024]{2,1,0:T(8,128)}, f32[2,128,153]{1,2,0:T(8,128)}) async-done(((f32[2,96,1024]{2,1,0:T(8,128)}, f32[2,128,153]{1,2,0:T(8,128)}), (f32[2,96,1024]{2,1,0:T(8,128)}, f32[2,128,153]{1,2,0:T(8,128)})) %all-reduce.9.cloned.1.call-update) | async-done | bytes 943120 | tf_op jit(solution)/shard_map/psum | solution.py:98
  852.3 2.1 slice_bitcast_fusion
  (94 shorter events, 10.9 us)
Async XLA Ops:
  7.2 42.8 %copy-start = (bf16[96,1024]{1,0:T(8,128)(2,1)S(1)}, bf16[96,1024]{1,0:T(8,128)(2,1)}, u32[]{:S(2)}) copy-start(bf16[96,1024]{1,0:T(8,128)(2,1)} %param.17) | copy-start | bytes 589828
  7.2 128.7 %all-reduce.5.cloned.1.call-start = ((), (), s32[]{:S(2)}) async-start(), calls=%async_computation.2 | async-start | bytes 1048576 | tf_op jit(solution)/shard_map/psum | solution.py:35
  7.2 1.2 copy-start.8
  49.9 0.9 copy-start.2
  51.9 0.7 copy-start.6
  51.9 0.8 copy-start.5
  52.7 0.9 copy-start.1
  53.5 1.0 copy-start.4
  53.5 1.0 copy-start.7
  55.7 24.5 %all-to-all-start.1 = ((bf16[128,64,4]{0,2,1:T(4,128)(2,1)}), bf16[128,64,4]{0,2,1:T(4,128)(2,1)S(1)}, u32[]{:S(2)}, u32[]{:S(2)}) async-start(bf16[128,64,4]{0,2,1:T(4,128)(2,1)} %bitcast.18), calls=%async_computation.1 | async-start | bytes 131072 | tf_op jit(solution)/shard_map/all_to_all | solution.py:86
  153.3 21.6 %all-to-all-start = ((bf16[128,64,4]{0,2,1:T(4,128)(2,1)}), bf16[128,64,4]{0,2,1:T(4,128)(2,1)S(1)}, u32[]{:S(2)}, u32[]{:S(2)}) async-start(bf16[128,64,4]{0,2,1:T(4,128)(2,1)} %bitcast.1), calls=%async_computation | async-start | bytes 131072 | tf_op jit(solution)/shard_map/all_to_all | solution.py:47
  165.3 77.0 %all-reduce.7.cloned.1.call-start = ((), (), s32[]{:S(2)}) async-start(), calls=%async_computation.3 | async-start | bytes 163840 | tf_op jit(solution)/shard_map/psum | solution.py:67
  177.4 674.8 %all-reduce.9.cloned.1.call-start = ((), (), s32[]{:S(2)}) async-start(), calls=%async_computation.4 | async-start | bytes 1900544 | tf_op jit(solution)/shard_map/psum | solution.py:98
  852.3 2.1 copy-start.3
Sparse Core Ops, SparseCore 0:
  52.1 83.7 all-reduce.4
  177.6 64.7 all-reduce.6
  246.0 606.2 all-reduce.8
where the time goes:
time: 863 us; the launch traced here: 862 us
  waiting for transfers between devices  746 us (86%)
  local copies, waits for them, and re-layouts  29.1 us (3%)
  starting transfers between devices  27.1 us (3%)
  other arithmetic  23.5 us (3%)
  blocking collectives  15.3 us (2%)
  between operations  13.9 us (2%)
    psum x1, waiting for transfers between devices, local(): lower_grads, upper_terms = lax.psum((lower_grads, upper_terms), 'nodes')  608 us
    psum x1, waiting for transfers between devices, local(): lax.psum(logit_part.astype(jnp.bfloat16), 'feat').astype(jnp.float32)  64.2 us
    psum x1, waiting for transfers between devices, local(): lax.psum((result + lax.dot_general(w1_neigh, agg_one, weight_rows, prefer...  55.7 us
    gather x25, local copies, waits for them, and re-layouts, add_neighbour(): return running + features[neighbour_rows].astype(jnp.float32)  21.3 us
    select_n x25, other arithmetic, add_neighbour(): return running + features[neighbour_rows].astype(jnp.float32)  17.7 us
  transfers between devices with their start and end apart: 5, of which 5 were waited for; matrix products, arithmetic and copies ran while one was open for 1% of the time, Pallas kernels for 0%

commit v1 on v0

v1 whole, which is shorter than its diff:
```python
import jax
import jax.numpy as jnp
from jax import lax
from jax.experimental import pallas as pl
from jax.experimental.pallas import tpu as pltpu
from jax.sharding import PartitionSpec as P

BF = jnp.bfloat16
F32 = jnp.float32
MESH = pl.DeviceIdType.MESH

TGT = 256
ND = 1024
FSL = 96
HID = 1024
HS = 128
C = 153
K1 = 25
K2 = 15
CP = 192
LP = 5
Q = 8
PIECE = 48
SETS = ((0, 2), (2, 2), (4, 1))


def dot(a, b):
    return jnp.dot(a, b, preferred_element_type=F32)


def dot_dims(a, b, ca, cb):
    return lax.dot_general(a, b, (((ca,), (cb,)), ((), ())), preferred_element_type=F32)


def main_kernel(
    features_hbm, near_hbm, tid_hbm, sid_hbm, snear_hbm,
    w1s_hbm, w1n_hbm, w2s_hbm, w2n_hbm, lg_hbm,
    gath, lout,
    feat_v, near_v, tid_v, sid_v, snear_v, w1_v, w2s_v, w2n_v, lg_v,
    keys, tally, sel, x_v, xt, seedtally, lgp, w2c, perm,
    pair_src, pair_rcv, p_own, rs_src, relay_rcv, rs_rcv,
    bz_src, bz_rcv, bw_src, bw_rcv, dt, d_hid,
    fw_src, fw_rcv, fz_src, fz_rcv,
    ag, gst, rw_rcv, zsrc, z_rcv, zc_rcv, zfull, lst, l_rcv, ltot,
    in_sem, out_sem, pair_s, pair_r, rs_s, rs_r, bz_s, bz_r, bw_s, bw_r,
    fw_s, fw_r, fz_s, fz_r, ag_s, ag_r, agf_s, agf_r,
    rw_s, rw_r, z_s, z_r, az_s, az_r, aw_s, aw_r, l_s, l_r, la_s, la_r,
):
    node = lax.axis_index("nodes")
    f = lax.axis_index("feat")
    z = node // Q
    w = node % Q
    h = f // 2
    c = f % 2

    def z_peer(d):
        zz = lax.rem(z + d, Q)
        return zz, (zz * Q + w, f)

    def w_peer(d):
        ww = lax.rem(w + d, Q)
        return ww, (z * Q + ww, f)

    def f_peer(d):
        ff = lax.rem(f + d, Q)
        return ff, (node, ff)

    partner = (node, h * 2 + (1 - c))

    up = (node, lax.rem(h + 1, 4) * 2 + c)
    down = (node, lax.rem(h + 3, 4) * 2 + c)

    def each(body):
        def step(d, carry):
            body(d)
            return carry

        lax.fori_loop(1, Q, step, 0)

    barrier = pltpu.get_barrier_semaphore()

    def greet(d):
        for where in (z_peer(d)[1], w_peer(d)[1], f_peer(d)[1]):
            pl.semaphore_signal(barrier, inc=1, device_id=where, device_id_type=MESH)

    each(greet)

    loads = [
        pltpu.make_async_copy(src, dst, in_sem.at[n])
        for n, (src, dst) in enumerate(
            (
                (snear_hbm, snear_v),
                (sid_hbm, sid_v),
                (lg_hbm, lg_v),
                (w2s_hbm, w2s_v),
                (w2n_hbm, w2n_v),
                (near_hbm, near_v),
                (tid_hbm, tid_v),
                (features_hbm, feat_v),
                (w1s_hbm, w1_v.at[pl.ds(0, FSL)]),
                (w1n_hbm, w1_v.at[pl.ds(FSL, FSL)]),
            )
        )
    ]
    for load in loads:
        load.start()

    pending = []

    def remote(src, dst, s_sem, r_sem, where):
        return pltpu.make_async_remote_copy(
            src_ref=src, dst_ref=dst, send_sem=s_sem, recv_sem=r_sem,
            device_id=where, device_id_type=MESH,
        )

    def send(*args):
        copy = remote(*args)
        copy.start()
        pending.append(copy.wait_send)

    def send_each(copy_of, test_of=None):
        def start(d):
            if test_of is None:
                copy_of(d).start()
            else:
                pl.when(test_of(d))(lambda: copy_of(d).start())

        def finish(d):
            if test_of is None:
                copy_of(d).wait_send()
            else:
                pl.when(test_of(d))(lambda: copy_of(d).wait_send())

        each(start)
        pending.append(lambda: each(finish))

    def sent():
        for finish in pending:
            finish()
        pending.clear()

    def landed(ref, r_sem):
        pltpu.make_async_copy(ref, ref, r_sem).wait()

    one = jnp.ones((16, 128), BF)
    zero = jnp.zeros((16, 128), BF)
    row = lax.broadcasted_iota(jnp.int32, (16, 128), 0)

    def key_of(ids):
        return lax.shift_left(128 + (ids & 127), lax.shift_right_logical(ids, 7)).astype(F32)

    def spread(first, ids):
        for k in range(ids.shape[0]):
            keys[first + k] = jnp.broadcast_to(ids[k:k + 1], (16, TGT)).astype(BF)

    def count(fan, row_key, totals_of, ones_of):
        def body(step, carry):
            mine = [row_key(step * 64 + j * 16 + row).astype(BF) for j in range(4)]
            for half in range(2):
                cols = slice(half * 128, half * 128 + 128)
                totals = [zero] * 4
                for k in range(fan):
                    theirs = keys[k, :, cols]
                    totals = [t + jnp.where(theirs == m, one, zero) for t, m in zip(totals, mine)]
                theirs = keys[fan, :, cols]
                for j in range(4):
                    rows = pl.ds(pl.multiple_of(step * 64 + j * 16, 16), 16)
                    totals_of[rows, cols] = totals[j]
                    ones_of[rows, cols] = jnp.where(theirs == mine[j], one, zero)
            return carry

        return body

    def swap(n):
        return ((n >> 2) & 7) * 32 + (n >> 5) * 4 + (n & 3)

    a = lax.broadcasted_iota(jnp.int32, (TGT, TGT), 0)
    b = lax.broadcasted_iota(jnp.int32, (TGT, TGT), 1)
    perm[...] = jnp.where(swap(a) == b, 1.0, 0.0).astype(BF)

    for n in range(5):
        loads[n].wait()
    for padded, first, given in ((lgp, 0, lg_v), (w2c, 0, w2s_v), (w2c, CP, w2n_v)):
        padded[first:first + CP] = jnp.zeros((CP, padded.shape[1]), BF)
        padded[first:first + C] = given[...]
    spread(0, snear_v[...].astype(F32))
    spread(K2, sid_v[...].astype(F32))
    lax.fori_loop(
        0, TGT // 64, count(K2, lambda n: swap(n).astype(F32), seedtally.at[1], seedtally.at[0]), 0
    )
    lg = lgp[...].astype(F32).T.astype(BF)
    back = jnp.concatenate([dot(seedtally[0], lg), dot(seedtally[1], lg) / K2], axis=1)
    bw_src[...] = back.astype(BF).reshape(Q, 32, 2 * CP)

    def to_w(src, dst, s_sem, r_sem):
        def copy_of(d):
            ww, where = w_peer(d)
            return remote(src.at[ww], dst.at[w], s_sem.at[d - 1], r_sem.at[d - 1], where)

        send_each(copy_of)
        dst[w] = src[w]

    def to_z(src, dst, s_sem, r_sem):
        def copy_of(d):
            zz, where = z_peer(d)
            return remote(src.at[zz], dst.at[z], s_sem.at[d - 1], r_sem.at[d - 1], where)

        send_each(copy_of)
        dst[z] = src[z]

    def from_w(dst, r_sem):
        each(lambda d: landed(dst.at[lax.rem(w + Q - d, Q)], r_sem.at[d - 1]))

    def from_z(dst, r_sem):
        each(lambda d: landed(dst.at[lax.rem(z + Q - d, Q)], r_sem.at[d - 1]))

    pl.semaphore_wait(barrier, 3 * (Q - 1))
    to_w(bw_src, bw_rcv, bw_s, bw_r)

    loads[5].wait()
    loads[6].wait()
    spread(0, key_of(near_v[...]))
    spread(K1, key_of(tid_v[...]))
    lax.fori_loop(0, ND // 64, count(K1, key_of, tally, sel), 0)

    loads[7].wait()
    x_self = (dot(feat_v[...], sel[...])).astype(BF)
    agg = (dot(feat_v[...], tally[...]) / K1).astype(BF)
    xt[0:FSL] = x_self
    xt[FSL:2 * FSL] = agg
    x_v[...] = jnp.concatenate([x_self.astype(F32), agg.astype(F32)], axis=0).T.astype(BF)

    loads[8].wait()
    loads[9].wait()

    def partial(dh, cc):
        col = pl.ds(pl.multiple_of((lax.rem(h + dh, 4) * 2 + cc) * HS, HS), HS)
        return dot(x_v[...], w1_v[:, col])

    for dh in (2, 1, 3, 0):
        pair_src[dh] = partial(dh, 1 - c).astype(BF)
        send(pair_src.at[dh], pair_rcv.at[dh], pair_s.at[dh], pair_r.at[dh], partner)
    for dh in (2, 1, 3, 0):
        p_own[dh] = partial(dh, c)
    from_w(bw_rcv, bw_r)
    turned = dot(perm[...], bw_rcv[...].reshape(TGT, 2 * CP)).astype(BF)
    bz_src[...] = turned.reshape(Q, 32, 2 * CP)
    to_z(bz_src, bz_rcv, bz_s, bz_r)

    lo, hi = pl.ds(0, 128), pl.ds(128, 128)
    landed(pair_rcv.at[2], pair_r.at[2])
    rs_src[0] = (p_own[2] + pair_rcv[2].astype(F32)).astype(BF)
    send(rs_src.at[0, lo], relay_rcv.at[0], rs_s.at[0], rs_r.at[0], up)
    send(rs_src.at[0, hi], relay_rcv.at[1], rs_s.at[1], rs_r.at[1], down)
    landed(pair_rcv.at[1], pair_r.at[1])
    rs_src[1, 128:256] = (p_own[1, 128:256] + pair_rcv[1, 128:256].astype(F32)).astype(BF)
    send(rs_src.at[1, hi], rs_rcv.at[0, hi], rs_s.at[2], rs_r.at[2], up)
    landed(pair_rcv.at[3], pair_r.at[3])
    rs_src[2, 0:128] = (p_own[3, 0:128] + pair_rcv[3, 0:128].astype(F32)).astype(BF)
    send(rs_src.at[2, lo], rs_rcv.at[1, lo], rs_s.at[3], rs_r.at[3], down)
    landed(relay_rcv.at[0], rs_r.at[0])
    rs_src[1, 0:128] = (
        p_own[1, 0:128] + pair_rcv[1, 0:128].astype(F32) + relay_rcv[0].astype(F32)
    ).astype(BF)
    send(rs_src.at[1, lo], rs_rcv.at[0, lo], rs_s.at[4], rs_r.at[4], up)
    landed(relay_rcv.at[1], rs_r.at[1])
    rs_src[2, 128:256] = (
        p_own[3, 128:256] + pair_rcv[3, 128:256].astype(F32) + relay_rcv[1].astype(F32)
    ).astype(BF)
    send(rs_src.at[2, hi], rs_rcv.at[1, hi], rs_s.at[5], rs_r.at[5], down)

    from_z(bz_rcv, bz_r)
    back = bz_rcv[...].reshape(TGT, 2 * CP)
    d_hid[...] = dot(back, w2c[...])
    dt[...] = back.astype(F32).T.astype(BF)

    landed(pair_rcv.at[0], pair_r.at[0])
    pre = p_own[0] + pair_rcv[0].astype(F32)
    landed(rs_rcv.at[0, hi], rs_r.at[2])
    landed(rs_rcv.at[1, lo], rs_r.at[3])
    landed(rs_rcv.at[0, lo], rs_r.at[4])
    landed(rs_rcv.at[1, hi], rs_r.at[5])
    pre = pre + rs_rcv[0].astype(F32) + rs_rcv[1].astype(F32)
    sigma = 1.0 / (1.0 + jnp.exp(-pre))
    ag[0, 0] = (d_hid[...] * (sigma * (1.0 + pre * (1.0 - sigma)))).astype(BF)
    send(ag.at[0, 0, lo], ag.at[3, 0, lo], ag_s.at[0], ag_r.at[0], up)
    send(ag.at[0, 0, hi], ag.at[1, 0, hi], ag_s.at[1], ag_r.at[1], down)
    send(ag.at[0, 0], ag.at[0, 1], agf_s.at[0], agf_r.at[0], partner)
    send(ag.at[0, 0, hi], ag.at[3, 0, hi], ag_s.at[2], ag_r.at[2], up)
    send(ag.at[0, 0, lo], ag.at[1, 0, lo], ag_s.at[3], ag_r.at[3], down)
    hidden = (pre * sigma).astype(BF)
    fz_src[...] = hidden.reshape(Q, 32, HS)
    to_z(fz_src, fz_rcv, fz_s, fz_r)
    gst[:, 0] = dot(dt[...], hidden).astype(BF).reshape(Q, PIECE, HS)

    slots = {0: 1, 1: 2, 3: 3, 2: 4}

    def lower(dh, dc):
        grad = dot(xt[...], ag[dh, dc]).astype(BF).reshape(4, PIECE, HS)
        cc = c if dc == 0 else 1 - c
        gst[pl.ds(cc * 4, 4), slots[dh]] = grad

    def scatter(n):
        span = pl.ds(*SETS[n])

        def copy_of(d):
            ww, where = w_peer(d)
            return remote(
                gst.at[ww, span], rw_rcv.at[d - 1, span], rw_s.at[n, d - 1], rw_r.at[n, d - 1], where
            )

        send_each(copy_of)

    def reduce_w(n):
        first, many = SETS[n]
        each(lambda d: landed(rw_rcv.at[d - 1, pl.ds(first, many)], rw_r.at[n, d - 1]))
        for slot in range(first, first + many):
            total = gst[w, slot].astype(F32)
            for d in range(1, Q):
                total = total + rw_rcv[d - 1, slot].astype(F32)
            zsrc[slot * 3:slot * 3 + 3] = total.astype(BF).reshape(3, 16, HS)

    def owned(n, zz):
        lo, hi = SETS[n][0] * 3, (SETS[n][0] + SETS[n][1]) * 3
        k = lo + lax.rem(zz + 16 - lo % Q, Q)
        return k < hi, jnp.minimum(k, hi - 1)

    def scatter_z(n):
        reduce_w(n)

        def copy_of(d):
            zz, where = z_peer(d)
            k = owned(n, zz)[1]
            return remote(zsrc.at[k], z_rcv.at[n, d - 1], z_s.at[n, d - 1], z_r.at[n, d - 1], where)

        send_each(copy_of, lambda d: owned(n, z_peer(d)[0])[0])

    def gather_z(n):
        test, k = owned(n, z)

        @pl.when(test)
        def _():
            each(lambda d: landed(z_rcv.at[n, d - 1], z_r.at[n, d - 1]))
            total = zsrc[k].astype(F32)
            for d in range(1, Q):
                total = total + z_rcv[n, d - 1].astype(F32)
            zfull[k] = total.astype(BF)

        def copy_of(d):
            return remote(zfull.at[k], zfull.at[k], az_s.at[n, d - 1], az_r.at[n, d - 1], z_peer(d)[1])

        send_each(copy_of, lambda d: test)

    def gather_w(n):
        pieces = pl.ds(SETS[n][0] * 3, SETS[n][1] * 3)

        def wait(d):
            test, k = owned(n, lax.rem(z + Q - d, Q))
            pl.when(test)(lambda: landed(zfull.at[k], az_r.at[n, d - 1]))

        if n < 2:
            each(wait)

        def copy_of(d):
            return remote(
                zfull.at[pieces], gath.at[w, pieces], aw_s.at[n, d - 1], aw_r.at[n, d - 1], w_peer(d)[1]
            )

        send_each(copy_of)
        pltpu.make_async_copy(zfull.at[pieces], gath.at[w, pieces], out_sem.at[n]).start()

    last = pl.ds(12, 3)

    def exchange_z():
        reduce_w(2)

        def copy_of(d):
            return remote(zsrc.at[last], zc_rcv.at[z], z_s.at[2, d - 1], z_r.at[2, d - 1], z_peer(d)[1])

        send_each(copy_of)
        zc_rcv[z] = zsrc[12:15]

    def sum_z():
        from_z(zc_rcv, z_r.at[2])
        total = zc_rcv[0].astype(F32)
        for zz in range(1, Q):
            total = total + zc_rcv[zz].astype(F32)
        zfull[12:15] = total.astype(BF)

    lower(0, 0)
    landed(ag.at[0, 1], agf_r.at[0])
    lower(0, 1)
    scatter(0)

    landed(ag.at[3, 0, lo], ag_r.at[0])
    send(ag.at[3, 0, lo], ag.at[2, 0, lo], ag_s.at[4], ag_r.at[4], up)
    landed(ag.at[1, 0, hi], ag_r.at[1])
    send(ag.at[1, 0, hi], ag.at[2, 0, hi], ag_s.at[5], ag_r.at[5], down)
    landed(ag.at[3, 0, hi], ag_r.at[2])
    send(ag.at[3, 0], ag.at[3, 1], agf_s.at[3], agf_r.at[3], partner)
    landed(ag.at[1, 0, lo], ag_r.at[3])
    send(ag.at[1, 0], ag.at[1, 1], agf_s.at[1], agf_r.at[1], partner)
    lower(3, 0)
    lower(1, 0)

    from_z(fz_rcv, fz_r)
    fw_src[...] = dot(perm[...], fz_rcv[...].reshape(TGT, HS)).astype(BF).reshape(Q, 32, HS)
    to_w(fw_src, fw_rcv, fw_s, fw_r)

    scatter_z(0)
    landed(ag.at[3, 1], agf_r.at[3])
    lower(3, 1)
    landed(ag.at[1, 1], agf_r.at[1])
    lower(1, 1)
    scatter(1)
    landed(ag.at[2, 0, lo], ag_r.at[4])
    landed(ag.at[2, 0, hi], ag_r.at[5])
    send(ag.at[2, 0], ag.at[2, 1], agf_s.at[2], agf_r.at[2], partner)
    lower(2, 0)
    gather_z(0)
    landed(ag.at[2, 1], agf_r.at[2])
    lower(2, 1)
    scatter(2)
    scatter_z(1)

    from_w(fw_rcv, fw_r)
    received = fw_rcv[...].reshape(TGT, HS).astype(F32).T.astype(BF)
    h_self = dot(received, seedtally[0]).astype(BF)
    agg_two = (dot(received, seedtally[1]) / K2).astype(BF)
    part = dot(w2c[0:CP], h_self) + dot(w2c[CP:2 * CP], agg_two)
    lst[...] = part[0:LP * 32].astype(BF).reshape(LP, 32, TGT)

    def logit_part(d):
        ff, where = f_peer(d)
        return remote(lst.at[lax.rem(ff, LP)], l_rcv.at[d - 1], l_s.at[d - 1], l_r.at[d - 1], where)

    send_each(logit_part, lambda d: f_peer(d)[0] < LP)

    gather_w(0)
    exchange_z()
    gather_z(1)

    fl = lax.rem(f, LP)

    @pl.when(f < LP)
    def _():
        each(lambda d: landed(l_rcv.at[d - 1], l_r.at[d - 1]))
        total = lst[fl].astype(F32)
        for d in range(1, Q):
            total = total + l_rcv[d - 1].astype(F32)
        ltot[...] = total.astype(BF)
        pltpu.make_async_copy(ltot, lout.at[fl], out_sem.at[3]).start()

    def logit_sum(d):
        return remote(ltot, lout.at[fl], la_s.at[d - 1], la_r.at[d - 1], f_peer(d)[1])

    send_each(logit_sum, lambda d: f < LP)

    gather_w(1)
    sum_z()
    gather_w(2)
    sent()

    def logits_in(d):
        ff = lax.rem(f + Q - d, Q)
        pl.when(ff < LP)(lambda: landed(lout.at[lax.rem(ff, LP)], la_r.at[d - 1]))

    each(logits_in)

    @pl.when(f < LP)
    def _():
        landed(lout.at[fl], out_sem.at[3])

    for n, (first, many) in enumerate(SETS):
        pieces = pl.ds(first * 3, many * 3)
        each(lambda d: landed(gath.at[lax.rem(w + Q - d, Q), pieces], aw_r.at[n, d - 1]))
        landed(gath.at[w, pieces], out_sem.at[n])


def finish_kernel(gath, lout, logits, g1s, g1n, g2s, g2n):
    h = lax.axis_index("feat") // 2
    logits[...] = lout[...].reshape(LP * 32, TGT)[0:C].astype(F32)
    for ww in range(Q):
        cc, k = ww // 4, ww % 4
        mine = gath[ww].reshape(5 * PIECE, HS).astype(F32)
        out = g2s if ww < 4 else g2n
        count = min(PIECE, C - k * PIECE)
        out[k * PIECE:k * PIECE + count] = mine[0:count]
        out = g1s if k < 2 else g1n
        for slot, dh in ((1, 0), (2, 1), (3, 3), (4, 2)):
            col = pl.ds(pl.multiple_of((2 * lax.rem(h + dh, 4) + cc) * HS, HS), HS)
            out[(k % 2) * PIECE:(k % 2 + 1) * PIECE, col] = mine[slot * PIECE:(slot + 1) * PIECE]


def local(
    features, target_ids, near_ids, seed_ids, seed_near, w1_self, w1_neigh, w2_self, w2_neigh, logit_grad
):
    vm = pltpu.VMEM
    dma = pltpu.SemaphoreType.DMA
    vspec = pl.BlockSpec(memory_space=pltpu.VMEM)
    hspec = pl.BlockSpec(memory_space=pltpu.HBM)
    blocks = vm((Q, 32, HS), BF)
    wide = vm((Q, 32, 2 * CP), BF)
    scratch = [
        vm((FSL, ND), BF), vm((K1, TGT), jnp.int32), vm((1, TGT), jnp.int32), vm((1, TGT), jnp.int32),
        vm((K2, TGT), jnp.int32), vm((2 * FSL, HID), BF), vm((C, HS), BF), vm((C, HS), BF), vm((C, TGT), BF),
        vm((K1 + 1, 16, TGT), BF), vm((ND, TGT), BF), vm((ND, TGT), BF), vm((TGT, 2 * FSL), BF),
        vm((2 * FSL, TGT), BF), vm((2, TGT, TGT), BF), vm((CP, TGT), BF), vm((2 * CP, HS), BF), vm((TGT, TGT), BF),
        vm((4, TGT, HS), BF), vm((4, TGT, HS), BF), vm((4, TGT, HS), F32), vm((3, TGT, HS), BF),
        vm((2, 128, HS), BF), vm((2, TGT, HS), BF),
        wide, wide, wide, wide, vm((2 * CP, TGT), BF), vm((TGT, HS), F32),
        blocks, blocks, blocks, blocks,
        vm((4, 2, TGT, HS), BF), vm((Q, 5, PIECE, HS), BF), vm((Q - 1, 5, PIECE, HS), BF),
        vm((15, 16, HS), BF), vm((2, Q - 1, 16, HS), BF), vm((Q, 3, 16, HS), BF), vm((15, 16, HS), BF),
        vm((LP, 32, TGT), BF), vm((Q - 1, 32, TGT), BF), vm((32, TGT), BF),
        dma((10,)), dma((4,)), dma((4,)), dma((4,)), dma((6,)), dma((6,)),
        dma((7,)), dma((7,)), dma((7,)), dma((7,)), dma((7,)), dma((7,)), dma((7,)), dma((7,)),
        dma((6,)), dma((6,)), dma((4,)), dma((4,)),
        dma((3, 7)), dma((3, 7)), dma((3, 7)), dma((3, 7)), dma((3, 7)), dma((3, 7)), dma((3, 7)), dma((3, 7)),
        dma((7,)), dma((7,)), dma((7,)), dma((7,)),
    ]
    gath, lout = pl.pallas_call(
        main_kernel,
        out_shape=(
            jax.ShapeDtypeStruct((Q, 15, 16, HS), BF),
            jax.ShapeDtypeStruct((LP, 32, TGT), BF),
        ),
        in_specs=[hspec] * 10,
        out_specs=(hspec, hspec),
        scratch_shapes=scratch,
        compiler_params=pltpu.CompilerParams(
            collective_id=0, has_side_effects=True, vmem_limit_bytes=62 * 1024 * 1024
        ),
        name="sage_step",
    )(
        features.T, near_ids.T, target_ids.reshape(1, TGT), seed_ids.reshape(1, TGT), seed_near.T,
        w1_self, w1_neigh, w2_self.T, w2_neigh.T, logit_grad.T,
    )
    logits, g1s, g1n, g2s, g2n = pl.pallas_call(
        finish_kernel,
        out_shape=(
            jax.ShapeDtypeStruct((C, TGT), F32),
            jax.ShapeDtypeStruct((FSL, HID), F32),
            jax.ShapeDtypeStruct((FSL, HID), F32),
            jax.ShapeDtypeStruct((C, HS), F32),
            jax.ShapeDtypeStruct((C, HS), F32),
        ),
        in_specs=[vspec, vspec],
        out_specs=(vspec,) * 5,
        compiler_params=pltpu.CompilerParams(vmem_limit_bytes=62 * 1024 * 1024),
        name="finish",
    )(gath, lout)
    return logits.T, g1s, g1n, g2s.T, g2n.T


def solution(mesh):
    return jax.shard_map(
        local,
        mesh=mesh,
        in_specs=(
            P("nodes", "feat"),
            P("nodes"),
            P("nodes", None),
            P("nodes"),
            P("nodes", None),
            P("feat", None),
            P("feat", None),
            P("feat", None),
            P("feat", None),
            P("nodes", None),
        ),
        out_specs=(
            P("nodes", None),
            P("feat", None),
            P("feat", None),
            P("feat", None),
            P("feat", None),
        ),
        check_vma=False,
    )
```

time: 863 us -> 61 us (0.07)
  the two profiles are of different devices: /device:TPU:2 before, /device:TPU:1 now
where the time goes in v1:
time: 61 us; the launch traced here: 60.8 us
  Pallas kernels  60.1 us (99%)
  between operations  0.64 us (1%)
    pallas_call x1, Pallas kernels, local(): pl.pallas_call(main_kernel, out_shape=(jax.ShapeDtypeStruct((Q, 15, 16, H...  58.1 us
    pallas_call x1, Pallas kernels, local(): pl.pallas_call(finish_kernel, out_shape=(jax.ShapeDtypeStruct((C, TGT), F...  2.06 us

profile of v1, /device:TPU:1, one launch (start us, length us, event | category | flops | bytes accessed | tf_op | source)
XLA Modules:
  0.0 60.8 jit_solution(8160743735417962026)
XLA Ops:
  0.6 58.1 %sage_step.1 = (bf16[8,15,16,128]{3,2,1,0:T(8,128)(2,1)}, bf16[5,32,256]{2,1,0:T(8,128)(2,1)}) custom-call(bf16[96,1024]{1,0:T(8,128)(2,1)} %bitcast.11, s32[25,256]{1,0:T(8,128)} %bitcast.15, s32[1,256]{1,0:T(1,128)} %bitcast.17, s32[1,256]{1,0:T(1,128)} %bitcast.18, s32[15,256]{1,0:T(8,128)} %bitcast.16, bf16[96,1024]{1,0:T(8,128)(2,1)} %w1s_hbm.1, ...), custom_call_target="tpu_custom_call" | custom-call | tf_op jit(solution)/shard_map/sage_step/pallas_call | solution.py:522
  58.7 2.1 %finish.1 = (f32[153,256]{1,0:T(8,128)}, f32[96,1024]{1,0:T(8,128)}, f32[96,1024]{1,0:T(8,128)}, f32[153,128]{1,0:T(8,128)}, f32[153,128]{1,0:T(8,128)}) custom-call(bf16[8,15,16,128]{3,2,1,0:T(8,128)(2,1)} %get-tuple-element.12.gath, bf16[5,32,256]{2,1,0:T(8,128)(2,1)} %get-tuple-element.13.lout), custom_call_target="tpu_custom_call" | custom-call | tf_op jit(solution)/shard_map/finish/pallas_call | solution.py:539

commit v2 on v1

--- a/solution.py
+++ b/solution.py
@@ -142,34 +142,47 @@
     def landed(ref, r_sem):
         pltpu.make_async_copy(ref, ref, r_sem).wait()
 
-    one = jnp.ones((16, 128), BF)
-    zero = jnp.zeros((16, 128), BF)
-    row = lax.broadcasted_iota(jnp.int32, (16, 128), 0)
-
-    def key_of(ids):
-        return lax.shift_left(128 + (ids & 127), lax.shift_right_logical(ids, 7)).astype(F32)
-
-    def spread(first, ids):
-        for k in range(ids.shape[0]):
-            keys[first + k] = jnp.broadcast_to(ids[k:k + 1], (16, TGT)).astype(BF)
-
-    def count(fan, row_key, totals_of, ones_of):
+    row = lax.broadcasted_iota(jnp.int32, (8, 128), 0)
+
+    def count(ids, own, low, words, totals_of, ones_of):
+        fan = ids.shape[0]
+        high = lax.shift_right_logical(ids, low.bit_length() - 1)
+        digit = lax.shift_left(jnp.ones_like(ids), (high & 3) * 8)
+        tables = [ids & (low - 1)]
+        tables += [jnp.where((high >> 2) == g, digit, 0) for g in range(words)]
+        for n, table in enumerate(tables):
+            for k in range(fan):
+                keys[n, k] = jnp.broadcast_to(table[k:k + 1], (8, TGT))
+        keys[0, K1] = jnp.broadcast_to(own, (8, TGT))
+
         def body(step, carry):
-            mine = [row_key(step * 64 + j * 16 + row).astype(BF) for j in range(4)]
+            mine = [step * 32 + j * 8 + row for j in range(4)]
             for half in range(2):
                 cols = slice(half * 128, half * 128 + 128)
-                totals = [zero] * 4
+                totals = [[jnp.zeros((8, 128), jnp.int32)] * 4 for _ in range(words)]
                 for k in range(fan):
-                    theirs = keys[k, :, cols]
-                    totals = [t + jnp.where(theirs == m, one, zero) for t, m in zip(totals, mine)]
-                theirs = keys[fan, :, cols]
-                for j in range(4):
-                    rows = pl.ds(pl.multiple_of(step * 64 + j * 16, 16), 16)
-                    totals_of[rows, cols] = totals[j]
-                    ones_of[rows, cols] = jnp.where(theirs == mine[j], one, zero)
+                    theirs = keys[0, k, :, cols]
+                    hits = [theirs == m for m in mine]
+                    for g in range(words):
+                        word = keys[1 + g, k, :, cols]
+                        totals[g] = [t + jnp.where(hit, word, 0) for t, hit in zip(totals[g], hits)]
+                theirs = keys[0, K1, :, cols]
+                for part in range(4 * words):
+                    for j in (0, 2):
+                        first = part * low + step * 32 + j * 8
+                        rows = pl.ds(pl.multiple_of(first, 16), 16)
+                        both = [
+                            lax.shift_right_logical(totals[part // 4][n], 8 * (part % 4)) & 255
+                            for n in (j, j + 1)
+                        ]
+                        totals_of[rows, cols] = jnp.concatenate(both, axis=0).astype(F32).astype(BF)
+                        both = [
+                            jnp.where(theirs == mine[n] + part * low, 1.0, 0.0) for n in (j, j + 1)
+                        ]
+                        ones_of[rows, cols] = jnp.concatenate(both, axis=0).astype(BF)
             return carry
 
-        return body
+        lax.fori_loop(0, low // 32, body, 0)
 
     def swap(n):
         return ((n >> 2) & 7) * 32 + (n >> 5) * 4 + (n & 3)
@@ -183,11 +196,7 @@
     for padded, first, given in ((lgp, 0, lg_v), (w2c, 0, w2s_v), (w2c, CP, w2n_v)):
         padded[first:first + CP] = jnp.zeros((CP, padded.shape[1]), BF)
         padded[first:first + C] = given[...]
-    spread(0, snear_v[...].astype(F32))
-    spread(K2, sid_v[...].astype(F32))
-    lax.fori_loop(
-        0, TGT // 64, count(K2, lambda n: swap(n).astype(F32), seedtally.at[1], seedtally.at[0]), 0
-    )
+    count(swap(snear_v[...]), swap(sid_v[...]), 64, 1, seedtally.at[1], seedtally.at[0])
     lg = lgp[...].astype(F32).T.astype(BF)
     back = jnp.concatenate([dot(seedtally[0], lg), dot(seedtally[1], lg) / K2], axis=1)
     bw_src[...] = back.astype(BF).reshape(Q, 32, 2 * CP)
@@ -219,9 +228,7 @@
 
     loads[5].wait()
     loads[6].wait()
-    spread(0, key_of(near_v[...]))
-    spread(K1, key_of(tid_v[...]))
-    lax.fori_loop(0, ND // 64, count(K1, key_of, tally, sel), 0)
+    count(near_v[...], tid_v[...], 128, 2, tally, sel)
 
     loads[7].wait()
     x_self = (dot(feat_v[...], sel[...])).astype(BF)
@@ -504,7 +511,7 @@
     scratch = [
         vm((FSL, ND), BF), vm((K1, TGT), jnp.int32), vm((1, TGT), jnp.int32), vm((1, TGT), jnp.int32),
         vm((K2, TGT), jnp.int32), vm((2 * FSL, HID), BF), vm((C, HS), BF), vm((C, HS), BF), vm((C, TGT), BF),
-        vm((K1 + 1, 16, TGT), BF), vm((ND, TGT), BF), vm((ND, TGT), BF), vm((TGT, 2 * FSL), BF),
+        vm((3, K1 + 1, 8, TGT), jnp.int32), vm((ND, TGT), BF), vm((ND, TGT), BF), vm((TGT, 2 * FSL), BF),
         vm((2 * FSL, TGT), BF), vm((2, TGT, TGT), BF), vm((CP, TGT), BF), vm((2 * CP, HS), BF), vm((TGT, TGT), BF),
         vm((4, TGT, HS), BF), vm((4, TGT, HS), BF), vm((4, TGT, HS), F32), vm((3, TGT, HS), BF),
         vm((2, 128, HS), BF), vm((2, TGT, HS), BF),

time: 61 us -> 61.9 us (1.015)
  Pallas kernels: 60.1 us -> 61.1 us
    pallas_call x1, Pallas kernels: 58.1 us -> 59 us  [local(): pl.pallas_call(main_kernel, out_shape=(jax.ShapeDtypeStruct((Q, 15, 16, H...]
where the time goes in v2:
time: 61.9 us; the launch traced here: 61.7 us
  Pallas kernels  61.1 us (99%)
  between operations  0.64 us (1%)
    pallas_call x1, Pallas kernels, local(): pl.pallas_call(main_kernel, out_shape=(jax.ShapeDtypeStruct((Q, 15, 16, H...  59 us
    pallas_call x1, Pallas kernels, local(): pl.pallas_call(finish_kernel, out_shape=(jax.ShapeDtypeStruct((C, TGT), F...  2.06 us

profile of v2, /device:TPU:1, one launch (start us, length us, event | category | flops | bytes accessed | tf_op | source)
XLA Modules:
  0.0 61.7 jit_solution(11746374546550545129)
XLA Ops:
  0.6 59.0 %sage_step.1 = (bf16[8,15,16,128]{3,2,1,0:T(8,128)(2,1)}, bf16[5,32,256]{2,1,0:T(8,128)(2,1)}) custom-call(bf16[96,1024]{1,0:T(8,128)(2,1)} %bitcast.11, s32[25,256]{1,0:T(8,128)} %bitcast.15, s32[1,256]{1,0:T(1,128)} %bitcast.17, s32[1,256]{1,0:T(1,128)} %bitcast.18, s32[15,256]{1,0:T(8,128)} %bitcast.16, bf16[96,1024]{1,0:T(8,128)(2,1)} %w1s_hbm.1, ...), custom_call_target="tpu_custom_call" | custom-call | tf_op jit(solution)/shard_map/sage_step/pallas_call | solution.py:529
  59.6 2.1 %finish.1 = (f32[153,256]{1,0:T(8,128)}, f32[96,1024]{1,0:T(8,128)}, f32[96,1024]{1,0:T(8,128)}, f32[153,128]{1,0:T(8,128)}, f32[153,128]{1,0:T(8,128)}) custom-call(bf16[8,15,16,128]{3,2,1,0:T(8,128)(2,1)} %get-tuple-element.12.gath, bf16[5,32,256]{2,1,0:T(8,128)(2,1)} %get-tuple-element.13.lout), custom_call_target="tpu_custom_call" | custom-call | tf_op jit(solution)/shard_map/finish/pallas_call | solution.py:546

commit v3 on v2

--- a/solution.py
+++ b/solution.py
@@ -54,16 +54,13 @@
     c = f % 2
 
     def z_peer(d):
-        zz = lax.rem(z + d, Q)
-        return zz, (zz * Q + w, f)
+        return z ^ d, (node ^ (d * Q), f)
 
     def w_peer(d):
-        ww = lax.rem(w + d, Q)
-        return ww, (z * Q + ww, f)
+        return w ^ d, (node ^ d, f)
 
     def f_peer(d):
-        ff = lax.rem(f + d, Q)
-        return ff, (node, ff)
+        return f ^ d, (node, f ^ d)
 
     partner = (node, h * 2 + (1 - c))
 
@@ -71,11 +68,8 @@
     down = (node, lax.rem(h + 3, 4) * 2 + c)
 
     def each(body):
-        def step(d, carry):
+        for d in range(1, Q):
             body(d)
-            return carry
-
-        lax.fori_loop(1, Q, step, 0)
 
     barrier = pltpu.get_barrier_semaphore()
 
@@ -218,10 +212,10 @@
         dst[z] = src[z]
 
     def from_w(dst, r_sem):
-        each(lambda d: landed(dst.at[lax.rem(w + Q - d, Q)], r_sem.at[d - 1]))
+        each(lambda d: landed(dst.at[w ^ d], r_sem.at[d - 1]))
 
     def from_z(dst, r_sem):
-        each(lambda d: landed(dst.at[lax.rem(z + Q - d, Q)], r_sem.at[d - 1]))
+        each(lambda d: landed(dst.at[z ^ d], r_sem.at[d - 1]))
 
     pl.semaphore_wait(barrier, 3 * (Q - 1))
     to_w(bw_src, bw_rcv, bw_s, bw_r)
@@ -325,48 +319,36 @@
             total = gst[w, slot].astype(F32)
             for d in range(1, Q):
                 total = total + rw_rcv[d - 1, slot].astype(F32)
-            zsrc[slot * 3:slot * 3 + 3] = total.astype(BF).reshape(3, 16, HS)
-
-    def owned(n, zz):
-        lo, hi = SETS[n][0] * 3, (SETS[n][0] + SETS[n][1]) * 3
-        k = lo + lax.rem(zz + 16 - lo % Q, Q)
-        return k < hi, jnp.minimum(k, hi - 1)
+            piece = 8 * n + 3 * (slot - first)
+            zsrc[piece:piece + 3] = total.astype(BF).reshape(3, 16, HS)
 
     def scatter_z(n):
         reduce_w(n)
+        zsrc[8 * n + 6:8 * n + 8] = jnp.zeros((2, 16, HS), BF)
 
         def copy_of(d):
             zz, where = z_peer(d)
-            k = owned(n, zz)[1]
-            return remote(zsrc.at[k], z_rcv.at[n, d - 1], z_s.at[n, d - 1], z_r.at[n, d - 1], where)
-
-        send_each(copy_of, lambda d: owned(n, z_peer(d)[0])[0])
+            return remote(zsrc.at[8 * n + zz], z_rcv.at[n, d - 1], z_s.at[n, d - 1], z_r.at[n, d - 1], where)
+
+        send_each(copy_of)
 
     def gather_z(n):
-        test, k = owned(n, z)
-
-        @pl.when(test)
-        def _():
-            each(lambda d: landed(z_rcv.at[n, d - 1], z_r.at[n, d - 1]))
-            total = zsrc[k].astype(F32)
-            for d in range(1, Q):
-                total = total + z_rcv[n, d - 1].astype(F32)
-            zfull[k] = total.astype(BF)
+        k = 8 * n + z
+        each(lambda d: landed(z_rcv.at[n, d - 1], z_r.at[n, d - 1]))
+        total = zsrc[k].astype(F32)
+        for d in range(1, Q):
+            total = total + z_rcv[n, d - 1].astype(F32)
+        zfull[k] = total.astype(BF)
 
         def copy_of(d):
             return remote(zfull.at[k], zfull.at[k], az_s.at[n, d - 1], az_r.at[n, d - 1], z_peer(d)[1])
 
-        send_each(copy_of, lambda d: test)
+        send_each(copy_of)
 
     def gather_w(n):
-        pieces = pl.ds(SETS[n][0] * 3, SETS[n][1] * 3)
-
-        def wait(d):
-            test, k = owned(n, lax.rem(z + Q - d, Q))
-            pl.when(test)(lambda: landed(zfull.at[k], az_r.at[n, d - 1]))
-
+        pieces = pl.ds(8 * n, 3 * SETS[n][1])
         if n < 2:
-            each(wait)
+            each(lambda d: landed(zfull.at[8 * n + (z ^ d)], az_r.at[n, d - 1]))
 
         def copy_of(d):
             return remote(
@@ -376,7 +358,7 @@
         send_each(copy_of)
         pltpu.make_async_copy(zfull.at[pieces], gath.at[w, pieces], out_sem.at[n]).start()
 
-    last = pl.ds(12, 3)
+    last = pl.ds(16, 3)
 
     def exchange_z():
         reduce_w(2)
@@ -385,14 +367,14 @@
             return remote(zsrc.at[last], zc_rcv.at[z], z_s.at[2, d - 1], z_r.at[2, d - 1], z_peer(d)[1])
 
         send_each(copy_of)
-        zc_rcv[z] = zsrc[12:15]
+        zc_rcv[z] = zsrc[16:19]
 
     def sum_z():
         from_z(zc_rcv, z_r.at[2])
         total = zc_rcv[0].astype(F32)
         for zz in range(1, Q):
             total = total + zc_rcv[zz].astype(F32)
-        zfull[12:15] = total.astype(BF)
+        zfull[16:19] = total.astype(BF)
 
     lower(0, 0)
     landed(ag.at[0, 1], agf_r.at[0])
@@ -469,7 +451,7 @@
     sent()
 
     def logits_in(d):
-        ff = lax.rem(f + Q - d, Q)
+        ff = f ^ d
         pl.when(ff < LP)(lambda: landed(lout.at[lax.rem(ff, LP)], la_r.at[d - 1]))
 
     each(logits_in)
@@ -479,8 +461,8 @@
         landed(lout.at[fl], out_sem.at[3])
 
     for n, (first, many) in enumerate(SETS):
-        pieces = pl.ds(first * 3, many * 3)
-        each(lambda d: landed(gath.at[lax.rem(w + Q - d, Q), pieces], aw_r.at[n, d - 1]))
+        pieces = pl.ds(8 * n, many * 3)
+        each(lambda d: landed(gath.at[w ^ d, pieces], aw_r.at[n, d - 1]))
         landed(gath.at[w, pieces], out_sem.at[n])
 
 
@@ -489,14 +471,14 @@
     logits[...] = lout[...].reshape(LP * 32, TGT)[0:C].astype(F32)
     for ww in range(Q):
         cc, k = ww // 4, ww % 4
-        mine = gath[ww].reshape(5 * PIECE, HS).astype(F32)
+        mine = gath[ww].reshape(19 * 16, HS).astype(F32)
         out = g2s if ww < 4 else g2n
         count = min(PIECE, C - k * PIECE)
         out[k * PIECE:k * PIECE + count] = mine[0:count]
         out = g1s if k < 2 else g1n
-        for slot, dh in ((1, 0), (2, 1), (3, 3), (4, 2)):
+        for first, dh in ((48, 0), (128, 1), (176, 3), (256, 2)):
             col = pl.ds(pl.multiple_of((2 * lax.rem(h + dh, 4) + cc) * HS, HS), HS)
-            out[(k % 2) * PIECE:(k % 2 + 1) * PIECE, col] = mine[slot * PIECE:(slot + 1) * PIECE]
+            out[(k % 2) * PIECE:(k % 2 + 1) * PIECE, col] = mine[first:first + PIECE]
 
 
 def local(
@@ -518,7 +500,7 @@
         wide, wide, wide, wide, vm((2 * CP, TGT), BF), vm((TGT, HS), F32),
         blocks, blocks, blocks, blocks,
         vm((4, 2, TGT, HS), BF), vm((Q, 5, PIECE, HS), BF), vm((Q - 1, 5, PIECE, HS), BF),
-        vm((15, 16, HS), BF), vm((2, Q - 1, 16, HS), BF), vm((Q, 3, 16, HS), BF), vm((15, 16, HS), BF),
+        vm((19, 16, HS), BF), vm((2, Q - 1, 16, HS), BF), vm((Q, 3, 16, HS), BF), vm((19, 16, HS), BF),
         vm((LP, 32, TGT), BF), vm((Q - 1, 32, TGT), BF), vm((32, TGT), BF),
         dma((10,)), dma((4,)), dma((4,)), dma((4,)), dma((6,)), dma((6,)),
         dma((7,)), dma((7,)), dma((7,)), dma((7,)), dma((7,)), dma((7,)), dma((7,)), dma((7,)),
@@ -529,7 +511,7 @@
     gath, lout = pl.pallas_call(
         main_kernel,
         out_shape=(
-            jax.ShapeDtypeStruct((Q, 15, 16, HS), BF),
+            jax.ShapeDtypeStruct((Q, 19, 16, HS), BF),
             jax.ShapeDtypeStruct((LP, 32, TGT), BF),
         ),
         in_specs=[hspec] * 10,

time: 61.9 us -> 61.8 us (level)
  Pallas kernels: 61.1 us -> 60.4 us
    pallas_call x1, Pallas kernels: 59 us -> 58.3 us  [local(): pl.pallas_call(main_kernel, out_shape=(jax.ShapeDtypeStruct((Q, 19, 16, H...]
where the time goes in v3:
time: 61.8 us; the launch traced here: 61 us
  Pallas kernels  60.4 us (98%)
  between operations  0.64 us (1%)
    pallas_call x1, Pallas kernels, local(): pl.pallas_call(main_kernel, out_shape=(jax.ShapeDtypeStruct((Q, 19, 16, H...  58.3 us
    pallas_call x1, Pallas kernels, local(): pl.pallas_call(finish_kernel, out_shape=(jax.ShapeDtypeStruct((C, TGT), F...  2.11 us

profile of v3, /device:TPU:1, one launch (start us, length us, event | category | flops | bytes accessed | tf_op | source)
XLA Modules:
  0.0 61.0 jit_solution(7283699846758880695)
XLA Ops:
  0.6 58.3 %sage_step.1 = (bf16[8,19,16,128]{3,2,1,0:T(8,128)(2,1)}, bf16[5,32,256]{2,1,0:T(8,128)(2,1)}) custom-call(bf16[96,1024]{1,0:T(8,128)(2,1)} %bitcast.11, s32[25,256]{1,0:T(8,128)} %bitcast.15, s32[1,256]{1,0:T(1,128)} %bitcast.17, s32[1,256]{1,0:T(1,128)} %bitcast.18, s32[15,256]{1,0:T(8,128)} %bitcast.16, bf16[96,1024]{1,0:T(8,128)(2,1)} %w1s_hbm.1, ...), custom_call_target="tpu_custom_call" | custom-call | tf_op jit(solution)/shard_map/sage_step/pallas_call | solution.py:511
  58.9 2.1 %finish.1 = (f32[153,256]{1,0:T(8,128)}, f32[96,1024]{1,0:T(8,128)}, f32[96,1024]{1,0:T(8,128)}, f32[153,128]{1,0:T(8,128)}, f32[153,128]{1,0:T(8,128)}) custom-call(bf16[8,19,16,128]{3,2,1,0:T(8,128)(2,1)} %get-tuple-element.12.gath, bf16[5,32,256]{2,1,0:T(8,128)(2,1)} %get-tuple-element.13.lout), custom_call_target="tpu_custom_call" | custom-call | tf_op jit(solution)/shard_map/finish/pallas_call | solution.py:528

commit v4 on v3

--- a/solution.py
+++ b/solution.py
@@ -21,7 +21,8 @@
 LP = 5
 Q = 8
 PIECE = 48
-SETS = ((0, 2), (2, 2), (4, 1))
+SETS = ((0, 1), (1, 2), (3, 1))
+WIDTHS = (6, 6, 3)
 
 
 def dot(a, b):
@@ -38,13 +39,13 @@
     gath, lout,
     feat_v, near_v, tid_v, sid_v, snear_v, w1_v, w2s_v, w2n_v, lg_v,
     keys, tally, sel, x_v, xt, seedtally, lgp, w2c, perm,
-    pair_src, pair_rcv, p_own, rs_src, relay_rcv, rs_rcv,
-    bz_src, bz_rcv, bw_src, bw_rcv, dt, d_hid,
+    w1_p, p_own, rs_src, relay_rcv, rs_rcv,
+    bw_src, bw_rcv, bz_src, bz_rcv, ew_src, ew_rcv, ez_src, ez_rcv,
     fw_src, fw_rcv, fz_src, fz_rcv,
-    ag, gst, rw_rcv, zsrc, z_rcv, zc_rcv, zfull, lst, l_rcv, ltot,
-    in_sem, out_sem, pair_s, pair_r, rs_s, rs_r, bz_s, bz_r, bw_s, bw_r,
-    fw_s, fw_r, fz_s, fz_r, ag_s, ag_r, agf_s, agf_r,
-    rw_s, rw_r, z_s, z_r, az_s, az_r, aw_s, aw_r, l_s, l_r, la_s, la_r,
+    ag, gst, gup, rw_rcv, rg_rcv, zsrc, z_rcv, zc_rcv, zfull, lst, l_rcv, ltot,
+    in_sem, out_sem, fx_s, fx_r, wx_s, wx_r, rs_s, rs_r, bw_s, bw_r, bz_s, bz_r,
+    ew_s, ew_r, ez_s, ez_r, fw_s, fw_r, fz_s, fz_r, ag_s, ag_r,
+    rw_s, rw_r, rg_s, rg_r, z_s, z_r, az_s, az_r, aw_s, aw_r, l_s, l_r, la_s, la_r,
 ):
     node = lax.axis_index("nodes")
     f = lax.axis_index("feat")
@@ -59,6 +60,9 @@
     def w_peer(d):
         return w ^ d, (node ^ d, f)
 
+    def v_peer(d):
+        return w ^ d, (node ^ d, f ^ 1)
+
     def f_peer(d):
         return f ^ d, (node, f ^ d)
 
@@ -70,14 +74,6 @@
     def each(body):
         for d in range(1, Q):
             body(d)
-
-    barrier = pltpu.get_barrier_semaphore()
-
-    def greet(d):
-        for where in (z_peer(d)[1], w_peer(d)[1], f_peer(d)[1]):
-            pl.semaphore_signal(barrier, inc=1, device_id=where, device_id_type=MESH)
-
-    each(greet)
 
     loads = [
         pltpu.make_async_copy(src, dst, in_sem.at[n])
@@ -90,7 +86,7 @@
                 (w2n_hbm, w2n_v),
                 (near_hbm, near_v),
                 (tid_hbm, tid_v),
-                (features_hbm, feat_v),
+                (features_hbm, feat_v.at[c]),
                 (w1s_hbm, w1_v.at[pl.ds(0, FSL)]),
                 (w1n_hbm, w1_v.at[pl.ds(FSL, FSL)]),
             )
@@ -98,6 +94,14 @@
     ]
     for load in loads:
         load.start()
+
+    barrier = pltpu.get_barrier_semaphore()
+
+    def greet(d):
+        for where in (z_peer(d)[1], w_peer(d)[1], f_peer(d)[1], v_peer(d)[1]):
+            pl.semaphore_signal(barrier, inc=1, device_id=where, device_id_type=MESH)
+
+    each(greet)
 
     pending = []
 
@@ -178,12 +182,14 @@
 
         lax.fori_loop(0, low // 32, body, 0)
 
+    pl.semaphore_wait(barrier, 4 * (Q - 1))
+    send(features_hbm, feat_v.at[c], fx_s.at[0], fx_r.at[0], partner)
+
+    def cols_of(dh, cc):
+        return pl.ds(pl.multiple_of((lax.rem(h + dh, 4) * 2 + cc) * HS, HS), HS)
+
     def swap(n):
         return ((n >> 2) & 7) * 32 + (n >> 5) * 4 + (n & 3)
-
-    a = lax.broadcasted_iota(jnp.int32, (TGT, TGT), 0)
-    b = lax.broadcasted_iota(jnp.int32, (TGT, TGT), 1)
-    perm[...] = jnp.where(swap(a) == b, 1.0, 0.0).astype(BF)
 
     for n in range(5):
         loads[n].wait()
@@ -191,9 +197,11 @@
         padded[first:first + CP] = jnp.zeros((CP, padded.shape[1]), BF)
         padded[first:first + C] = given[...]
     count(swap(snear_v[...]), swap(sid_v[...]), 64, 1, seedtally.at[1], seedtally.at[0])
-    lg = lgp[...].astype(F32).T.astype(BF)
-    back = jnp.concatenate([dot(seedtally[0], lg), dot(seedtally[1], lg) / K2], axis=1)
-    bw_src[...] = back.astype(BF).reshape(Q, 32, 2 * CP)
+    back = jnp.concatenate(
+        [dot_dims(seedtally[0], lgp[...], 1, 1), dot_dims(seedtally[1], lgp[...], 1, 1) / K2], axis=1
+    ).astype(BF)
+    bw_src[...] = dot(back, w2c[...]).astype(BF).reshape(Q, 32, HS)
+    ew_src[...] = back.reshape(Q, 32, 2 * CP)
 
     def to_w(src, dst, s_sem, r_sem):
         def copy_of(d):
@@ -217,89 +225,81 @@
     def from_z(dst, r_sem):
         each(lambda d: landed(dst.at[z ^ d], r_sem.at[d - 1]))
 
-    pl.semaphore_wait(barrier, 3 * (Q - 1))
     to_w(bw_src, bw_rcv, bw_s, bw_r)
+    loads[8].wait()
+    loads[9].wait()
+    for place, dh in enumerate((2, 1, 3, 0)):
+        send(w1_v.at[:, cols_of(dh, 1 - c)], w1_p.at[place], wx_s.at[place], wx_r.at[place], partner)
+    to_w(ew_src, ew_rcv, ew_s, ew_r)
 
     loads[5].wait()
     loads[6].wait()
     count(near_v[...], tid_v[...], 128, 2, tally, sel)
 
     loads[7].wait()
-    x_self = (dot(feat_v[...], sel[...])).astype(BF)
-    agg = (dot(feat_v[...], tally[...]) / K1).astype(BF)
-    xt[0:FSL] = x_self
-    xt[FSL:2 * FSL] = agg
-    x_v[...] = jnp.concatenate([x_self.astype(F32), agg.astype(F32)], axis=0).T.astype(BF)
-
-    loads[8].wait()
-    loads[9].wait()
-
-    def partial(dh, cc):
-        col = pl.ds(pl.multiple_of((lax.rem(h + dh, 4) * 2 + cc) * HS, HS), HS)
-        return dot(x_v[...], w1_v[:, col])
-
-    for dh in (2, 1, 3, 0):
-        pair_src[dh] = partial(dh, 1 - c).astype(BF)
-        send(pair_src.at[dh], pair_rcv.at[dh], pair_s.at[dh], pair_r.at[dh], partner)
-    for dh in (2, 1, 3, 0):
-        p_own[dh] = partial(dh, c)
-    from_w(bw_rcv, bw_r)
-    turned = dot(perm[...], bw_rcv[...].reshape(TGT, 2 * CP)).astype(BF)
-    bz_src[...] = turned.reshape(Q, 32, 2 * CP)
-    to_z(bz_src, bz_rcv, bz_s, bz_r)
+    landed(feat_v.at[1 - c], fx_r.at[0])
+    both = feat_v[...].reshape(2 * FSL, ND)
+    x_self = dot(both, sel[...]).astype(BF)
+    agg = (dot(both, tally[...]) / K1).astype(BF)
+    for cc in range(2):
+        part = slice(cc * FSL, cc * FSL + FSL)
+        mine = jnp.concatenate([x_self[part], agg[part]], axis=0)
+        xt[cc] = mine
+        x_v[cc] = mine.astype(F32).T.astype(BF)
+
+    for place, dh in enumerate((2, 1, 3, 0)):
+        landed(w1_p.at[place], wx_r.at[place])
+        p_own[place] = dot(x_v[c], w1_v[:, cols_of(dh, c)]) + dot(x_v[1 - c], w1_p[place])
 
     lo, hi = pl.ds(0, 128), pl.ds(128, 128)
-    landed(pair_rcv.at[2], pair_r.at[2])
-    rs_src[0] = (p_own[2] + pair_rcv[2].astype(F32)).astype(BF)
+    rs_src[0] = p_own[0].astype(BF)
     send(rs_src.at[0, lo], relay_rcv.at[0], rs_s.at[0], rs_r.at[0], up)
     send(rs_src.at[0, hi], relay_rcv.at[1], rs_s.at[1], rs_r.at[1], down)
-    landed(pair_rcv.at[1], pair_r.at[1])
-    rs_src[1, 128:256] = (p_own[1, 128:256] + pair_rcv[1, 128:256].astype(F32)).astype(BF)
+    rs_src[1, 128:256] = p_own[1, 128:256].astype(BF)
     send(rs_src.at[1, hi], rs_rcv.at[0, hi], rs_s.at[2], rs_r.at[2], up)
-    landed(pair_rcv.at[3], pair_r.at[3])
-    rs_src[2, 0:128] = (p_own[3, 0:128] + pair_rcv[3, 0:128].astype(F32)).astype(BF)
+    rs_src[2, 0:128] = p_own[2, 0:128].astype(BF)
     send(rs_src.at[2, lo], rs_rcv.at[1, lo], rs_s.at[3], rs_r.at[3], down)
+
+    a = lax.broadcasted_iota(jnp.int32, (TGT, TGT), 0)
+    b = lax.broadcasted_iota(jnp.int32, (TGT, TGT), 1)
+    perm[...] = jnp.where(swap(a) == b, 1.0, 0.0).astype(BF)
+    from_w(bw_rcv, bw_r)
+    bz_src[...] = dot(perm[...], bw_rcv[...].reshape(TGT, HS)).astype(BF).reshape(Q, 32, HS)
+    to_z(bz_src, bz_rcv, bz_s, bz_r)
+    from_w(ew_rcv, ew_r)
+    turned = dot(perm[...], ew_rcv[...].reshape(TGT, 2 * CP)).astype(BF)
+    ez_src[...] = turned.reshape(Q, 32, 2 * CP)
+    to_z(ez_src, ez_rcv, ez_s, ez_r)
+
     landed(relay_rcv.at[0], rs_r.at[0])
-    rs_src[1, 0:128] = (
-        p_own[1, 0:128] + pair_rcv[1, 0:128].astype(F32) + relay_rcv[0].astype(F32)
-    ).astype(BF)
+    rs_src[1, 0:128] = (p_own[1, 0:128] + relay_rcv[0].astype(F32)).astype(BF)
     send(rs_src.at[1, lo], rs_rcv.at[0, lo], rs_s.at[4], rs_r.at[4], up)
     landed(relay_rcv.at[1], rs_r.at[1])
-    rs_src[2, 128:256] = (
-        p_own[3, 128:256] + pair_rcv[3, 128:256].astype(F32) + relay_rcv[1].astype(F32)
-    ).astype(BF)
+    rs_src[2, 128:256] = (p_own[2, 128:256] + relay_rcv[1].astype(F32)).astype(BF)
     send(rs_src.at[2, hi], rs_rcv.at[1, hi], rs_s.at[5], rs_r.at[5], down)
-
     from_z(bz_rcv, bz_r)
-    back = bz_rcv[...].reshape(TGT, 2 * CP)
-    d_hid[...] = dot(back, w2c[...])
-    dt[...] = back.astype(F32).T.astype(BF)
-
-    landed(pair_rcv.at[0], pair_r.at[0])
-    pre = p_own[0] + pair_rcv[0].astype(F32)
+
+    pre = p_own[3]
     landed(rs_rcv.at[0, hi], rs_r.at[2])
     landed(rs_rcv.at[1, lo], rs_r.at[3])
     landed(rs_rcv.at[0, lo], rs_r.at[4])
     landed(rs_rcv.at[1, hi], rs_r.at[5])
     pre = pre + rs_rcv[0].astype(F32) + rs_rcv[1].astype(F32)
     sigma = 1.0 / (1.0 + jnp.exp(-pre))
-    ag[0, 0] = (d_hid[...] * (sigma * (1.0 + pre * (1.0 - sigma)))).astype(BF)
-    send(ag.at[0, 0, lo], ag.at[3, 0, lo], ag_s.at[0], ag_r.at[0], up)
-    send(ag.at[0, 0, hi], ag.at[1, 0, hi], ag_s.at[1], ag_r.at[1], down)
-    send(ag.at[0, 0], ag.at[0, 1], agf_s.at[0], agf_r.at[0], partner)
-    send(ag.at[0, 0, hi], ag.at[3, 0, hi], ag_s.at[2], ag_r.at[2], up)
-    send(ag.at[0, 0, lo], ag.at[1, 0, lo], ag_s.at[3], ag_r.at[3], down)
-    hidden = (pre * sigma).astype(BF)
-    fz_src[...] = hidden.reshape(Q, 32, HS)
+    d_hidden = bz_rcv[...].reshape(TGT, HS).astype(F32)
+    ag[0] = (d_hidden * (sigma * (1.0 + pre * (1.0 - sigma)))).astype(BF)
+    send(ag.at[0, lo], ag.at[3, lo], ag_s.at[0], ag_r.at[0], up)
+    send(ag.at[0, hi], ag.at[1, hi], ag_s.at[1], ag_r.at[1], down)
+    send(ag.at[0, hi], ag.at[3, hi], ag_s.at[2], ag_r.at[2], up)
+    send(ag.at[0, lo], ag.at[1, lo], ag_s.at[3], ag_r.at[3], down)
+    fz_src[...] = (pre * sigma).astype(BF).reshape(Q, 32, HS)
     to_z(fz_src, fz_rcv, fz_s, fz_r)
-    gst[:, 0] = dot(dt[...], hidden).astype(BF).reshape(Q, PIECE, HS)
-
-    slots = {0: 1, 1: 2, 3: 3, 2: 4}
-
-    def lower(dh, dc):
-        grad = dot(xt[...], ag[dh, dc]).astype(BF).reshape(4, PIECE, HS)
-        cc = c if dc == 0 else 1 - c
-        gst[pl.ds(cc * 4, 4), slots[dh]] = grad
+
+    slots = {0: 0, 1: 1, 3: 2, 2: 3}
+
+    def lower(dh):
+        grad = dot(xt[...].reshape(4 * FSL, TGT), ag[dh])
+        gst[:, slots[dh]] = grad.astype(BF).reshape(Q, PIECE, HS)
 
     def scatter(n):
         span = pl.ds(*SETS[n])
@@ -311,6 +311,19 @@
             )
 
         send_each(copy_of)
+
+    def scatter_upper():
+        for kk in range(Q):
+            ww, cc = 4 * c + kk // 2, kk % 2
+            here = jnp.logical_and(w == ww, c == cc)
+            there = jnp.logical_not(here)
+            far = remote(
+                gup.at[kk], rg_rcv.at[w], rg_s.at[kk], rg_r.at[w], (node - w + ww, 2 * h + cc)
+            )
+            near = pltpu.make_async_copy(gup.at[kk], rg_rcv.at[w], rg_r.at[w])
+            pl.when(there)(far.start)
+            pl.when(here)(near.start)
+            pending.append(lambda there=there, far=far: pl.when(there)(far.wait_send))
 
     def reduce_w(n):
         first, many = SETS[n]
@@ -321,6 +334,13 @@
                 total = total + rw_rcv[d - 1, slot].astype(F32)
             piece = 8 * n + 3 * (slot - first)
             zsrc[piece:piece + 3] = total.astype(BF).reshape(3, 16, HS)
+        if n == 0:
+            for ww in range(Q):
+                landed(rg_rcv.at[ww], rg_r.at[ww])
+            total = rg_rcv[0].astype(F32)
+            for ww in range(1, Q):
+                total = total + rg_rcv[ww].astype(F32)
+            zsrc[3:6] = total.astype(BF).reshape(3, 16, HS)
 
     def scatter_z(n):
         reduce_w(n)
@@ -346,17 +366,23 @@
         send_each(copy_of)
 
     def gather_w(n):
-        pieces = pl.ds(8 * n, 3 * SETS[n][1])
+        pieces = pl.ds(8 * n, WIDTHS[n])
         if n < 2:
             each(lambda d: landed(zfull.at[8 * n + (z ^ d)], az_r.at[n, d - 1]))
+        cc, place = w // 4, c * 4 + w % 4
 
         def copy_of(d):
             return remote(
-                zfull.at[pieces], gath.at[w, pieces], aw_s.at[n, d - 1], aw_r.at[n, d - 1], w_peer(d)[1]
+                zfull.at[pieces], gath.at[place, pieces], aw_s.at[n, d], aw_r.at[n, place],
+                (node ^ d, 2 * h + cc),
             )
 
         send_each(copy_of)
-        pltpu.make_async_copy(zfull.at[pieces], gath.at[w, pieces], out_sem.at[n]).start()
+        far = copy_of(0)
+        near = pltpu.make_async_copy(zfull.at[pieces], gath.at[place, pieces], aw_r.at[n, place])
+        pl.when(c != cc)(far.start)
+        pl.when(c == cc)(near.start)
+        pending.append(lambda: pl.when(c != cc)(far.wait_send))
 
     last = pl.ds(16, 3)
 
@@ -376,40 +402,34 @@
             total = total + zc_rcv[zz].astype(F32)
         zfull[16:19] = total.astype(BF)
 
-    lower(0, 0)
-    landed(ag.at[0, 1], agf_r.at[0])
-    lower(0, 1)
+    lower(0)
     scatter(0)
 
-    landed(ag.at[3, 0, lo], ag_r.at[0])
-    send(ag.at[3, 0, lo], ag.at[2, 0, lo], ag_s.at[4], ag_r.at[4], up)
-    landed(ag.at[1, 0, hi], ag_r.at[1])
-    send(ag.at[1, 0, hi], ag.at[2, 0, hi], ag_s.at[5], ag_r.at[5], down)
-    landed(ag.at[3, 0, hi], ag_r.at[2])
-    send(ag.at[3, 0], ag.at[3, 1], agf_s.at[3], agf_r.at[3], partner)
-    landed(ag.at[1, 0, lo], ag_r.at[3])
-    send(ag.at[1, 0], ag.at[1, 1], agf_s.at[1], agf_r.at[1], partner)
-    lower(3, 0)
-    lower(1, 0)
+    landed(ag.at[3, lo], ag_r.at[0])
+    send(ag.at[3, lo], ag.at[2, lo], ag_s.at[4], ag_r.at[4], up)
+    landed(ag.at[1, hi], ag_r.at[1])
+    send(ag.at[1, hi], ag.at[2, hi], ag_s.at[5], ag_r.at[5], down)
+
+    from_z(ez_rcv, ez_r)
+    collected = ez_rcv[...].reshape(TGT, 2 * CP).astype(F32).T.astype(BF)
+    gup[...] = dot(collected, fz_src[...].reshape(TGT, HS)).astype(BF).reshape(Q, PIECE, HS)
+    scatter_upper()
+
+    landed(ag.at[3, hi], ag_r.at[2])
+    lower(3)
+    landed(ag.at[1, lo], ag_r.at[3])
+    lower(1)
+    scatter(1)
 
     from_z(fz_rcv, fz_r)
     fw_src[...] = dot(perm[...], fz_rcv[...].reshape(TGT, HS)).astype(BF).reshape(Q, 32, HS)
     to_w(fw_src, fw_rcv, fw_s, fw_r)
 
+    landed(ag.at[2, lo], ag_r.at[4])
+    landed(ag.at[2, hi], ag_r.at[5])
+    lower(2)
+    scatter(2)
     scatter_z(0)
-    landed(ag.at[3, 1], agf_r.at[3])
-    lower(3, 1)
-    landed(ag.at[1, 1], agf_r.at[1])
-    lower(1, 1)
-    scatter(1)
-    landed(ag.at[2, 0, lo], ag_r.at[4])
-    landed(ag.at[2, 0, hi], ag_r.at[5])
-    send(ag.at[2, 0], ag.at[2, 1], agf_s.at[2], agf_r.at[2], partner)
-    lower(2, 0)
-    gather_z(0)
-    landed(ag.at[2, 1], agf_r.at[2])
-    lower(2, 1)
-    scatter(2)
     scatter_z(1)
 
     from_w(fw_rcv, fw_r)
@@ -425,8 +445,8 @@
 
     send_each(logit_part, lambda d: f_peer(d)[0] < LP)
 
-    gather_w(0)
     exchange_z()
+    gather_z(0)
     gather_z(1)
 
     fl = lax.rem(f, LP)
@@ -445,6 +465,7 @@
 
     send_each(logit_sum, lambda d: f < LP)
 
+    gather_w(0)
     gather_w(1)
     sum_z()
     gather_w(2)
@@ -460,25 +481,26 @@
     def _():
         landed(lout.at[fl], out_sem.at[3])
 
-    for n, (first, many) in enumerate(SETS):
-        pieces = pl.ds(8 * n, many * 3)
-        each(lambda d: landed(gath.at[w ^ d, pieces], aw_r.at[n, d - 1]))
-        landed(gath.at[w, pieces], out_sem.at[n])
+    for n in range(3):
+        for place in range(Q):
+            landed(gath.at[place, pl.ds(8 * n, WIDTHS[n])], aw_r.at[n, place])
 
 
 def finish_kernel(gath, lout, logits, g1s, g1n, g2s, g2n):
     h = lax.axis_index("feat") // 2
     logits[...] = lout[...].reshape(LP * 32, TGT)[0:C].astype(F32)
-    for ww in range(Q):
-        cc, k = ww // 4, ww % 4
-        mine = gath[ww].reshape(19 * 16, HS).astype(F32)
-        out = g2s if ww < 4 else g2n
-        count = min(PIECE, C - k * PIECE)
-        out[k * PIECE:k * PIECE + count] = mine[0:count]
+    for place in range(Q):
+        cc, k = place // 4, place % 4
+        mine = gath[place].reshape(19 * 16, HS).astype(F32)
         out = g1s if k < 2 else g1n
-        for first, dh in ((48, 0), (128, 1), (176, 3), (256, 2)):
+        for first, dh in ((0, 0), (128, 1), (176, 3), (256, 2)):
             col = pl.ds(pl.multiple_of((2 * lax.rem(h + dh, 4) + cc) * HS, HS), HS)
             out[(k % 2) * PIECE:(k % 2 + 1) * PIECE, col] = mine[first:first + PIECE]
+        kk = 2 * k + cc
+        out = g2s if kk < 4 else g2n
+        first = (kk % 4) * PIECE
+        count = min(PIECE, C - first)
+        out[first:first + count] = mine[PIECE:PIECE + count]
 
 
 def local(
@@ -491,22 +513,24 @@
     blocks = vm((Q, 32, HS), BF)
     wide = vm((Q, 32, 2 * CP), BF)
     scratch = [
-        vm((FSL, ND), BF), vm((K1, TGT), jnp.int32), vm((1, TGT), jnp.int32), vm((1, TGT), jnp.int32),
+        vm((2, FSL, ND), BF), vm((K1, TGT), jnp.int32), vm((1, TGT), jnp.int32), vm((1, TGT), jnp.int32),
         vm((K2, TGT), jnp.int32), vm((2 * FSL, HID), BF), vm((C, HS), BF), vm((C, HS), BF), vm((C, TGT), BF),
-        vm((3, K1 + 1, 8, TGT), jnp.int32), vm((ND, TGT), BF), vm((ND, TGT), BF), vm((TGT, 2 * FSL), BF),
-        vm((2 * FSL, TGT), BF), vm((2, TGT, TGT), BF), vm((CP, TGT), BF), vm((2 * CP, HS), BF), vm((TGT, TGT), BF),
-        vm((4, TGT, HS), BF), vm((4, TGT, HS), BF), vm((4, TGT, HS), F32), vm((3, TGT, HS), BF),
+        vm((3, K1 + 1, 8, TGT), jnp.int32), vm((ND, TGT), BF), vm((ND, TGT), BF), vm((2, TGT, 2 * FSL), BF),
+        vm((2, 2 * FSL, TGT), BF), vm((2, TGT, TGT), BF), vm((CP, TGT), BF), vm((2 * CP, HS), BF),
+        vm((TGT, TGT), BF),
+        vm((4, 2 * FSL, HS), BF), vm((4, TGT, HS), F32), vm((3, TGT, HS), BF),
         vm((2, 128, HS), BF), vm((2, TGT, HS), BF),
-        wide, wide, wide, wide, vm((2 * CP, TGT), BF), vm((TGT, HS), F32),
+        blocks, blocks, blocks, blocks, wide, wide, wide, wide,
         blocks, blocks, blocks, blocks,
-        vm((4, 2, TGT, HS), BF), vm((Q, 5, PIECE, HS), BF), vm((Q - 1, 5, PIECE, HS), BF),
+        vm((4, TGT, HS), BF), vm((Q, 4, PIECE, HS), BF), vm((Q, PIECE, HS), BF),
+        vm((Q - 1, 4, PIECE, HS), BF), vm((Q, PIECE, HS), BF),
         vm((19, 16, HS), BF), vm((2, Q - 1, 16, HS), BF), vm((Q, 3, 16, HS), BF), vm((19, 16, HS), BF),
         vm((LP, 32, TGT), BF), vm((Q - 1, 32, TGT), BF), vm((32, TGT), BF),
-        dma((10,)), dma((4,)), dma((4,)), dma((4,)), dma((6,)), dma((6,)),
+        dma((10,)), dma((4,)), dma((1,)), dma((1,)), dma((4,)), dma((4,)), dma((6,)), dma((6,)),
         dma((7,)), dma((7,)), dma((7,)), dma((7,)), dma((7,)), dma((7,)), dma((7,)), dma((7,)),
-        dma((6,)), dma((6,)), dma((4,)), dma((4,)),
-        dma((3, 7)), dma((3, 7)), dma((3, 7)), dma((3, 7)), dma((3, 7)), dma((3, 7)), dma((3, 7)), dma((3, 7)),
-        dma((7,)), dma((7,)), dma((7,)), dma((7,)),
+        dma((7,)), dma((7,)), dma((7,)), dma((7,)), dma((6,)), dma((6,)),
+        dma((3, 7)), dma((3, 7)), dma((8,)), dma((8,)), dma((3, 7)), dma((3, 7)), dma((3, 7)), dma((3, 7)),
+        dma((3, 8)), dma((3, 8)), dma((7,)), dma((7,)), dma((7,)), dma((7,)),
     ]
     gath, lout = pl.pallas_call(
         main_kernel,

time: 61.8 us -> 60 us (0.971)
  Pallas kernels: 60.4 us -> 59.2 us
    pallas_call x1, Pallas kernels: 58.3 us -> 57.1 us  [local(): pl.pallas_call(main_kernel, out_shape=(jax.ShapeDtypeStruct((Q, 19, 16, H...]
where the time goes in v4:
time: 60 us; the launch traced here: 59.8 us
  Pallas kernels  59.2 us (99%)
  between operations  0.64 us (1%)
    pallas_call x1, Pallas kernels, local(): pl.pallas_call(main_kernel, out_shape=(jax.ShapeDtypeStruct((Q, 19, 16, H...  57.1 us
    pallas_call x1, Pallas kernels, local(): pl.pallas_call(finish_kernel, out_shape=(jax.ShapeDtypeStruct((C, TGT), F...  2.11 us

profile of v4, /device:TPU:1, one launch (start us, length us, event | category | flops | bytes accessed | tf_op | source)
XLA Modules:
  0.0 59.8 jit_solution(15137433426177175933)
XLA Ops:
  0.6 57.1 %sage_step.1 = (bf16[8,19,16,128]{3,2,1,0:T(8,128)(2,1)}, bf16[5,32,256]{2,1,0:T(8,128)(2,1)}) custom-call(bf16[96,1024]{1,0:T(8,128)(2,1)} %bitcast.11, s32[25,256]{1,0:T(8,128)} %bitcast.15, s32[1,256]{1,0:T(1,128)} %bitcast.17, s32[1,256]{1,0:T(1,128)} %bitcast.18, s32[15,256]{1,0:T(8,128)} %bitcast.16, bf16[96,1024]{1,0:T(8,128)(2,1)} %w1s_hbm.1, ...), custom_call_target="tpu_custom_call" | custom-call | tf_op jit(solution)/shard_map/sage_step/pallas_call | solution.py:535
  57.7 2.1 %finish.1 = (f32[153,256]{1,0:T(8,128)}, f32[96,1024]{1,0:T(8,128)}, f32[96,1024]{1,0:T(8,128)}, f32[153,128]{1,0:T(8,128)}, f32[153,128]{1,0:T(8,128)}) custom-call(bf16[8,19,16,128]{3,2,1,0:T(8,128)(2,1)} %get-tuple-element.12.gath, bf16[5,32,256]{2,1,0:T(8,128)(2,1)} %get-tuple-element.13.lout), custom_call_target="tpu_custom_call" | custom-call | tf_op jit(solution)/shard_map/finish/pallas_call | solution.py:552

commit v5 on v4

--- a/solution.py
+++ b/solution.py
@@ -18,7 +18,7 @@
 K1 = 25
 K2 = 15
 CP = 192
-LP = 5
+LR = 80
 Q = 8
 PIECE = 48
 SETS = ((0, 1), (1, 2), (3, 1))
@@ -42,10 +42,10 @@
     w1_p, p_own, rs_src, relay_rcv, rs_rcv,
     bw_src, bw_rcv, bz_src, bz_rcv, ew_src, ew_rcv, ez_src, ez_rcv,
     fw_src, fw_rcv, fz_src, fz_rcv,
-    ag, gst, gup, rw_rcv, rg_rcv, zsrc, z_rcv, zc_rcv, zfull, lst, l_rcv, ltot,
+    ag, gst, gup, rw_rcv, rg_rcv, zsrc, z_rcv, zc_rcv, zfull, lst, l_rcv, l_chip, ltot,
     in_sem, out_sem, fx_s, fx_r, wx_s, wx_r, rs_s, rs_r, bw_s, bw_r, bz_s, bz_r,
     ew_s, ew_r, ez_s, ez_r, fw_s, fw_r, fz_s, fz_r, ag_s, ag_r,
-    rw_s, rw_r, rg_s, rg_r, z_s, z_r, az_s, az_r, aw_s, aw_r, l_s, l_r, la_s, la_r,
+    rw_s, rw_r, rg_s, rg_r, z_s, z_r, az_s, az_r, aw_s, aw_r, l_s, l_r,
 ):
     node = lax.axis_index("nodes")
     f = lax.axis_index("feat")
@@ -63,13 +63,11 @@
     def v_peer(d):
         return w ^ d, (node ^ d, f ^ 1)
 
-    def f_peer(d):
-        return f ^ d, (node, f ^ d)
-
     partner = (node, h * 2 + (1 - c))
 
     up = (node, lax.rem(h + 1, 4) * 2 + c)
     down = (node, lax.rem(h + 3, 4) * 2 + c)
+    across = (node, lax.rem(h + 2, 4) * 2 + c)
 
     def each(body):
         for d in range(1, Q):
@@ -98,10 +96,12 @@
     barrier = pltpu.get_barrier_semaphore()
 
     def greet(d):
-        for where in (z_peer(d)[1], w_peer(d)[1], f_peer(d)[1], v_peer(d)[1]):
+        for where in (z_peer(d)[1], w_peer(d)[1], v_peer(d)[1]):
             pl.semaphore_signal(barrier, inc=1, device_id=where, device_id_type=MESH)
 
     each(greet)
+    for where in (partner, up, down, across):
+        pl.semaphore_signal(barrier, inc=1, device_id=where, device_id_type=MESH)
 
     pending = []
 
@@ -182,7 +182,7 @@
 
         lax.fori_loop(0, low // 32, body, 0)
 
-    pl.semaphore_wait(barrier, 4 * (Q - 1))
+    pl.semaphore_wait(barrier, 3 * (Q - 1) + 4)
     send(features_hbm, feat_v.at[c], fx_s.at[0], fx_r.at[0], partner)
 
     def cols_of(dh, cc):
@@ -247,18 +247,23 @@
         xt[cc] = mine
         x_v[cc] = mine.astype(F32).T.astype(BF)
 
-    for place, dh in enumerate((2, 1, 3, 0)):
+    lo, hi = pl.ds(0, 128), pl.ds(128, 128)
+
+    def form(place, dh):
         landed(w1_p.at[place], wx_r.at[place])
         p_own[place] = dot(x_v[c], w1_v[:, cols_of(dh, c)]) + dot(x_v[1 - c], w1_p[place])
 
-    lo, hi = pl.ds(0, 128), pl.ds(128, 128)
+    form(0, 2)
     rs_src[0] = p_own[0].astype(BF)
     send(rs_src.at[0, lo], relay_rcv.at[0], rs_s.at[0], rs_r.at[0], up)
     send(rs_src.at[0, hi], relay_rcv.at[1], rs_s.at[1], rs_r.at[1], down)
+    form(1, 1)
     rs_src[1, 128:256] = p_own[1, 128:256].astype(BF)
     send(rs_src.at[1, hi], rs_rcv.at[0, hi], rs_s.at[2], rs_r.at[2], up)
+    form(2, 3)
     rs_src[2, 0:128] = p_own[2, 0:128].astype(BF)
     send(rs_src.at[2, lo], rs_rcv.at[1, lo], rs_s.at[3], rs_r.at[3], down)
+    form(3, 0)
 
     a = lax.broadcasted_iota(jnp.int32, (TGT, TGT), 0)
     b = lax.broadcasted_iota(jnp.int32, (TGT, TGT), 1)
@@ -437,50 +442,35 @@
     h_self = dot(received, seedtally[0]).astype(BF)
     agg_two = (dot(received, seedtally[1]) / K2).astype(BF)
     part = dot(w2c[0:CP], h_self) + dot(w2c[CP:2 * CP], agg_two)
-    lst[...] = part[0:LP * 32].astype(BF).reshape(LP, 32, TGT)
-
-    def logit_part(d):
-        ff, where = f_peer(d)
-        return remote(lst.at[lax.rem(ff, LP)], l_rcv.at[d - 1], l_s.at[d - 1], l_r.at[d - 1], where)
-
-    send_each(logit_part, lambda d: f_peer(d)[0] < LP)
+    lst[...] = part[0:2 * LR].astype(BF).reshape(2, LR, TGT)
+    send(lst.at[1 - c], l_rcv, l_s.at[0], l_r.at[0], partner)
 
     exchange_z()
     gather_z(0)
     gather_z(1)
 
-    fl = lax.rem(f, LP)
-
-    @pl.when(f < LP)
-    def _():
-        each(lambda d: landed(l_rcv.at[d - 1], l_r.at[d - 1]))
-        total = lst[fl].astype(F32)
-        for d in range(1, Q):
-            total = total + l_rcv[d - 1].astype(F32)
-        ltot[...] = total.astype(BF)
-        pltpu.make_async_copy(ltot, lout.at[fl], out_sem.at[3]).start()
-
-    def logit_sum(d):
-        return remote(ltot, lout.at[fl], la_s.at[d - 1], la_r.at[d - 1], f_peer(d)[1])
-
-    send_each(logit_sum, lambda d: f < LP)
+    landed(l_rcv, l_r.at[0])
+    l_chip[h] = (lst[c].astype(F32) + l_rcv[...].astype(F32)).astype(BF)
+    for n, where in enumerate((up, down, across)):
+        send(l_chip.at[h], l_chip.at[h], l_s.at[n + 1], l_r.at[n + 1], where)
 
     gather_w(0)
+    for n, dh in enumerate((3, 1, 2)):
+        landed(l_chip.at[lax.rem(h + dh, 4)], l_r.at[n + 1])
+    total = l_chip[0].astype(F32)
+    for n in range(1, 4):
+        total = total + l_chip[n].astype(F32)
+    ltot[...] = total.astype(BF)
+    send(ltot, lout.at[c], l_s.at[4], l_r.at[4], partner)
+    own_logits = pltpu.make_async_copy(ltot, lout.at[c], out_sem.at[3])
+    own_logits.start()
     gather_w(1)
     sum_z()
     gather_w(2)
     sent()
 
-    def logits_in(d):
-        ff = f ^ d
-        pl.when(ff < LP)(lambda: landed(lout.at[lax.rem(ff, LP)], la_r.at[d - 1]))
-
-    each(logits_in)
-
-    @pl.when(f < LP)
-    def _():
-        landed(lout.at[fl], out_sem.at[3])
-
+    landed(lout.at[1 - c], l_r.at[4])
+    own_logits.wait()
     for n in range(3):
         for place in range(Q):
             landed(gath.at[place, pl.ds(8 * n, WIDTHS[n])], aw_r.at[n, place])
@@ -488,7 +478,7 @@
 
 def finish_kernel(gath, lout, logits, g1s, g1n, g2s, g2n):
     h = lax.axis_index("feat") // 2
-    logits[...] = lout[...].reshape(LP * 32, TGT)[0:C].astype(F32)
+    logits[...] = lout[...].reshape(2 * LR, TGT)[0:C].astype(F32)
     for place in range(Q):
         cc, k = place // 4, place % 4
         mine = gath[place].reshape(19 * 16, HS).astype(F32)
@@ -525,18 +515,18 @@
         vm((4, TGT, HS), BF), vm((Q, 4, PIECE, HS), BF), vm((Q, PIECE, HS), BF),
         vm((Q - 1, 4, PIECE, HS), BF), vm((Q, PIECE, HS), BF),
         vm((19, 16, HS), BF), vm((2, Q - 1, 16, HS), BF), vm((Q, 3, 16, HS), BF), vm((19, 16, HS), BF),
-        vm((LP, 32, TGT), BF), vm((Q - 1, 32, TGT), BF), vm((32, TGT), BF),
+        vm((2, LR, TGT), BF), vm((LR, TGT), BF), vm((4, LR, TGT), BF), vm((LR, TGT), BF),
         dma((10,)), dma((4,)), dma((1,)), dma((1,)), dma((4,)), dma((4,)), dma((6,)), dma((6,)),
         dma((7,)), dma((7,)), dma((7,)), dma((7,)), dma((7,)), dma((7,)), dma((7,)), dma((7,)),
         dma((7,)), dma((7,)), dma((7,)), dma((7,)), dma((6,)), dma((6,)),
         dma((3, 7)), dma((3, 7)), dma((8,)), dma((8,)), dma((3, 7)), dma((3, 7)), dma((3, 7)), dma((3, 7)),
-        dma((3, 8)), dma((3, 8)), dma((7,)), dma((7,)), dma((7,)), dma((7,)),
+        dma((3, 8)), dma((3, 8)), dma((5,)), dma((5,)),
     ]
     gath, lout = pl.pallas_call(
         main_kernel,
         out_shape=(
             jax.ShapeDtypeStruct((Q, 19, 16, HS), BF),
-            jax.ShapeDtypeStruct((LP, 32, TGT), BF),
+            jax.ShapeDtypeStruct((2, LR, TGT), BF),
         ),
         in_specs=[hspec] * 10,
         out_specs=(hspec, hspec),

time: 60 us -> 61 us (1.017)
  Pallas kernels: 59.2 us -> 60.2 us
    pallas_call x1, Pallas kernels: 57.1 us -> 58.1 us  [local(): pl.pallas_call(main_kernel, out_shape=(jax.ShapeDtypeStruct((Q, 19, 16, H...]
where the time goes in v5:
time: 61 us; the launch traced here: 60.8 us
  Pallas kernels  60.2 us (99%)
  between operations  0.64 us (1%)
    pallas_call x1, Pallas kernels, local(): pl.pallas_call(main_kernel, out_shape=(jax.ShapeDtypeStruct((Q, 19, 16, H...  58.1 us
    pallas_call x1, Pallas kernels, local(): pl.pallas_call(finish_kernel, out_shape=(jax.ShapeDtypeStruct((C, TGT), F...  2.11 us

profile of v5, /device:TPU:1, one launch (start us, length us, event | category | flops | bytes accessed | tf_op | source)
XLA Modules:
  0.0 60.8 jit_solution(4745240757184706803)
XLA Ops:
  0.6 58.1 %sage_step.1 = (bf16[8,19,16,128]{3,2,1,0:T(8,128)(2,1)}, bf16[2,80,256]{2,1,0:T(8,128)(2,1)}) custom-call(bf16[96,1024]{1,0:T(8,128)(2,1)} %bitcast.11, s32[25,256]{1,0:T(8,128)} %bitcast.15, s32[1,256]{1,0:T(1,128)} %bitcast.17, s32[1,256]{1,0:T(1,128)} %bitcast.18, s32[15,256]{1,0:T(8,128)} %bitcast.16, bf16[96,1024]{1,0:T(8,128)(2,1)} %w1s_hbm.1, ...), custom_call_target="tpu_custom_call" | custom-call | tf_op jit(solution)/shard_map/sage_step/pallas_call | solution.py:525
  58.7 2.1 %finish.1 = (f32[153,256]{1,0:T(8,128)}, f32[96,1024]{1,0:T(8,128)}, f32[96,1024]{1,0:T(8,128)}, f32[153,128]{1,0:T(8,128)}, f32[153,128]{1,0:T(8,128)}) custom-call(bf16[8,19,16,128]{3,2,1,0:T(8,128)(2,1)} %get-tuple-element.12.gath, bf16[2,80,256]{2,1,0:T(8,128)(2,1)} %get-tuple-element.13.lout), custom_call_target="tpu_custom_call" | custom-call | tf_op jit(solution)/shard_map/finish/pallas_call | solution.py:542

commit v6 on v4

--- a/solution.py
+++ b/solution.py
@@ -247,18 +247,23 @@
         xt[cc] = mine
         x_v[cc] = mine.astype(F32).T.astype(BF)
 
-    for place, dh in enumerate((2, 1, 3, 0)):
+    lo, hi = pl.ds(0, 128), pl.ds(128, 128)
+
+    def form(place, dh):
         landed(w1_p.at[place], wx_r.at[place])
         p_own[place] = dot(x_v[c], w1_v[:, cols_of(dh, c)]) + dot(x_v[1 - c], w1_p[place])
 
-    lo, hi = pl.ds(0, 128), pl.ds(128, 128)
+    form(0, 2)
     rs_src[0] = p_own[0].astype(BF)
     send(rs_src.at[0, lo], relay_rcv.at[0], rs_s.at[0], rs_r.at[0], up)
     send(rs_src.at[0, hi], relay_rcv.at[1], rs_s.at[1], rs_r.at[1], down)
+    form(1, 1)
     rs_src[1, 128:256] = p_own[1, 128:256].astype(BF)
     send(rs_src.at[1, hi], rs_rcv.at[0, hi], rs_s.at[2], rs_r.at[2], up)
+    form(2, 3)
     rs_src[2, 0:128] = p_own[2, 0:128].astype(BF)
     send(rs_src.at[2, lo], rs_rcv.at[1, lo], rs_s.at[3], rs_r.at[3], down)
+    form(3, 0)
 
     a = lax.broadcasted_iota(jnp.int32, (TGT, TGT), 0)
     b = lax.broadcasted_iota(jnp.int32, (TGT, TGT), 1)
@@ -410,11 +415,6 @@
     landed(ag.at[1, hi], ag_r.at[1])
     send(ag.at[1, hi], ag.at[2, hi], ag_s.at[5], ag_r.at[5], down)
 
-    from_z(ez_rcv, ez_r)
-    collected = ez_rcv[...].reshape(TGT, 2 * CP).astype(F32).T.astype(BF)
-    gup[...] = dot(collected, fz_src[...].reshape(TGT, HS)).astype(BF).reshape(Q, PIECE, HS)
-    scatter_upper()
-
     landed(ag.at[3, hi], ag_r.at[2])
     lower(3)
     landed(ag.at[1, lo], ag_r.at[3])
@@ -425,12 +425,15 @@
     fw_src[...] = dot(perm[...], fz_rcv[...].reshape(TGT, HS)).astype(BF).reshape(Q, 32, HS)
     to_w(fw_src, fw_rcv, fw_s, fw_r)
 
+    from_z(ez_rcv, ez_r)
+    collected = ez_rcv[...].reshape(TGT, 2 * CP).astype(F32).T.astype(BF)
+    gup[...] = dot(collected, fz_src[...].reshape(TGT, HS)).astype(BF).reshape(Q, PIECE, HS)
+    scatter_upper()
+
     landed(ag.at[2, lo], ag_r.at[4])
     landed(ag.at[2, hi], ag_r.at[5])
     lower(2)
     scatter(2)
-    scatter_z(0)
-    scatter_z(1)
 
     from_w(fw_rcv, fw_r)
     received = fw_rcv[...].reshape(TGT, HS).astype(F32).T.astype(BF)
@@ -445,9 +448,11 @@
 
     send_each(logit_part, lambda d: f_peer(d)[0] < LP)
 
+    scatter_z(1)
+    scatter_z(0)
     exchange_z()
+    gather_z(1)
     gather_z(0)
-    gather_z(1)
 
     fl = lax.rem(f, LP)
 
@@ -465,8 +470,8 @@
 
     send_each(logit_sum, lambda d: f < LP)
 
+    gather_w(1)
     gather_w(0)
-    gather_w(1)
     sum_z()
     gather_w(2)
     sent()

time: 60 us -> 62.2 us (1.037)
  Pallas kernels: 59.2 us -> 61.4 us
    pallas_call x1, Pallas kernels: 57.1 us -> 59.3 us  [local(): pl.pallas_call(main_kernel, out_shape=(jax.ShapeDtypeStruct((Q, 19, 16, H...]
where the time goes in v6:
time: 62.2 us; the launch traced here: 62 us
  Pallas kernels  61.4 us (99%)
  between operations  0.64 us (1%)
    pallas_call x1, Pallas kernels, local(): pl.pallas_call(main_kernel, out_shape=(jax.ShapeDtypeStruct((Q, 19, 16, H...  59.3 us
    pallas_call x1, Pallas kernels, local(): pl.pallas_call(finish_kernel, out_shape=(jax.ShapeDtypeStruct((C, TGT), F...  2.11 us

profile of v6, /device:TPU:1, one launch (start us, length us, event | category | flops | bytes accessed | tf_op | source)
XLA Modules:
  0.0 62.0 jit_solution(12291593810293157048)
XLA Ops:
  0.6 59.3 %sage_step.1 = (bf16[8,19,16,128]{3,2,1,0:T(8,128)(2,1)}, bf16[5,32,256]{2,1,0:T(8,128)(2,1)}) custom-call(bf16[96,1024]{1,0:T(8,128)(2,1)} %bitcast.11, s32[25,256]{1,0:T(8,128)} %bitcast.15, s32[1,256]{1,0:T(1,128)} %bitcast.17, s32[1,256]{1,0:T(1,128)} %bitcast.18, s32[15,256]{1,0:T(8,128)} %bitcast.16, bf16[96,1024]{1,0:T(8,128)(2,1)} %w1s_hbm.1, ...), custom_call_target="tpu_custom_call" | custom-call | tf_op jit(solution)/shard_map/sage_step/pallas_call | solution.py:540
  59.9 2.1 %finish.1 = (f32[153,256]{1,0:T(8,128)}, f32[96,1024]{1,0:T(8,128)}, f32[96,1024]{1,0:T(8,128)}, f32[153,128]{1,0:T(8,128)}, f32[153,128]{1,0:T(8,128)}) custom-call(bf16[8,19,16,128]{3,2,1,0:T(8,128)(2,1)} %get-tuple-element.12.gath, bf16[5,32,256]{2,1,0:T(8,128)(2,1)} %get-tuple-element.13.lout), custom_call_target="tpu_custom_call" | custom-call | tf_op jit(solution)/shard_map/finish/pallas_call | solution.py:557

commit v7 on v4

--- a/solution.py
+++ b/solution.py
@@ -247,9 +247,13 @@
         xt[cc] = mine
         x_v[cc] = mine.astype(F32).T.astype(BF)
 
-    for place, dh in enumerate((2, 1, 3, 0)):
+    for place in range(4):
         landed(w1_p.at[place], wx_r.at[place])
-        p_own[place] = dot(x_v[c], w1_v[:, cols_of(dh, c)]) + dot(x_v[1 - c], w1_p[place])
+    own_rows = jnp.concatenate([w1_v[:, cols_of(dh, c)] for dh in (2, 1, 3, 0)], axis=1)
+    partner_rows = jnp.concatenate([w1_p[place] for place in range(4)], axis=1)
+    partials = dot(x_v[c], own_rows) + dot(x_v[1 - c], partner_rows)
+    for place in range(4):
+        p_own[place] = partials[:, place * HS:(place + 1) * HS]
 
     lo, hi = pl.ds(0, 128), pl.ds(128, 128)
     rs_src[0] = p_own[0].astype(BF)
@@ -416,9 +420,10 @@
     scatter_upper()
 
     landed(ag.at[3, hi], ag_r.at[2])
-    lower(3)
     landed(ag.at[1, lo], ag_r.at[3])
-    lower(1)
+    grads = dot(xt[...].reshape(4 * FSL, TGT), jnp.concatenate([ag[3], ag[1]], axis=1)).astype(BF)
+    gst[:, slots[3]] = grads[:, 0:HS].reshape(Q, PIECE, HS)
+    gst[:, slots[1]] = grads[:, HS:2 * HS].reshape(Q, PIECE, HS)
     scatter(1)
 
     from_z(fz_rcv, fz_r)

time: 60 us -> 60.7 us (1.012)
  Pallas kernels: 59.2 us -> 60 us
    pallas_call x1, Pallas kernels: 57.1 us -> 57.8 us  [local(): pl.pallas_call(main_kernel, out_shape=(jax.ShapeDtypeStruct((Q, 19, 16, H...]
where the time goes in v7:
time: 60.7 us; the launch traced here: 60.6 us
  Pallas kernels  60 us (99%)
  between operations  0.64 us (1%)
    pallas_call x1, Pallas kernels, local(): pl.pallas_call(main_kernel, out_shape=(jax.ShapeDtypeStruct((Q, 19, 16, H...  57.8 us
    pallas_call x1, Pallas kernels, local(): pl.pallas_call(finish_kernel, out_shape=(jax.ShapeDtypeStruct((C, TGT), F...  2.11 us

profile of v7, /device:TPU:1, one launch (start us, length us, event | category | flops | bytes accessed | tf_op | source)
XLA Modules:
  0.0 60.6 jit_solution(10722826460869400211)
XLA Ops:
  0.6 57.8 %sage_step.1 = (bf16[8,19,16,128]{3,2,1,0:T(8,128)(2,1)}, bf16[5,32,256]{2,1,0:T(8,128)(2,1)}) custom-call(bf16[96,1024]{1,0:T(8,128)(2,1)} %bitcast.11, s32[25,256]{1,0:T(8,128)} %bitcast.15, s32[1,256]{1,0:T(1,128)} %bitcast.17, s32[1,256]{1,0:T(1,128)} %bitcast.18, s32[15,256]{1,0:T(8,128)} %bitcast.16, bf16[96,1024]{1,0:T(8,128)(2,1)} %w1s_hbm.1, ...), custom_call_target="tpu_custom_call" | custom-call | tf_op jit(solution)/shard_map/sage_step/pallas_call | solution.py:540
  58.5 2.1 %finish.1 = (f32[153,256]{1,0:T(8,128)}, f32[96,1024]{1,0:T(8,128)}, f32[96,1024]{1,0:T(8,128)}, f32[153,128]{1,0:T(8,128)}, f32[153,128]{1,0:T(8,128)}) custom-call(bf16[8,19,16,128]{3,2,1,0:T(8,128)(2,1)} %get-tuple-element.12.gath, bf16[5,32,256]{2,1,0:T(8,128)(2,1)} %get-tuple-element.13.lout), custom_call_target="tpu_custom_call" | custom-call | tf_op jit(solution)/shard_map/finish/pallas_call | solution.py:557

commit v8 on v7

--- a/solution.py
+++ b/solution.py
@@ -39,7 +39,7 @@
     gath, lout,
     feat_v, near_v, tid_v, sid_v, snear_v, w1_v, w2s_v, w2n_v, lg_v,
     keys, tally, sel, x_v, xt, seedtally, lgp, w2c, perm,
-    w1_p, p_own, rs_src, relay_rcv, rs_rcv,
+    w1_p, p_own, rs_src, rs_rcv,
     bw_src, bw_rcv, bz_src, bz_rcv, ew_src, ew_rcv, ez_src, ez_rcv,
     fw_src, fw_rcv, fz_src, fz_rcv,
     ag, gst, gup, rw_rcv, rg_rcv, zsrc, z_rcv, zc_rcv, zfull, lst, l_rcv, ltot,
@@ -70,6 +70,7 @@
 
     up = (node, lax.rem(h + 1, 4) * 2 + c)
     down = (node, lax.rem(h + 3, 4) * 2 + c)
+    across = (node, lax.rem(h + 2, 4) * 2 + c)
 
     def each(body):
         for d in range(1, Q):
@@ -255,14 +256,9 @@
     for place in range(4):
         p_own[place] = partials[:, place * HS:(place + 1) * HS]
 
-    lo, hi = pl.ds(0, 128), pl.ds(128, 128)
-    rs_src[0] = p_own[0].astype(BF)
-    send(rs_src.at[0, lo], relay_rcv.at[0], rs_s.at[0], rs_r.at[0], up)
-    send(rs_src.at[0, hi], relay_rcv.at[1], rs_s.at[1], rs_r.at[1], down)
-    rs_src[1, 128:256] = p_own[1, 128:256].astype(BF)
-    send(rs_src.at[1, hi], rs_rcv.at[0, hi], rs_s.at[2], rs_r.at[2], up)
-    rs_src[2, 0:128] = p_own[2, 0:128].astype(BF)
-    send(rs_src.at[2, lo], rs_rcv.at[1, lo], rs_s.at[3], rs_r.at[3], down)
+    for place, where in enumerate((across, up, down)):
+        rs_src[place] = p_own[place].astype(BF)
+        send(rs_src.at[place], rs_rcv.at[place], rs_s.at[place], rs_r.at[place], where)
 
     a = lax.broadcasted_iota(jnp.int32, (TGT, TGT), 0)
     b = lax.broadcasted_iota(jnp.int32, (TGT, TGT), 1)
@@ -275,27 +271,18 @@
     ez_src[...] = turned.reshape(Q, 32, 2 * CP)
     to_z(ez_src, ez_rcv, ez_s, ez_r)
 
-    landed(relay_rcv.at[0], rs_r.at[0])
-    rs_src[1, 0:128] = (p_own[1, 0:128] + relay_rcv[0].astype(F32)).astype(BF)
-    send(rs_src.at[1, lo], rs_rcv.at[0, lo], rs_s.at[4], rs_r.at[4], up)
-    landed(relay_rcv.at[1], rs_r.at[1])
-    rs_src[2, 128:256] = (p_own[2, 128:256] + relay_rcv[1].astype(F32)).astype(BF)
-    send(rs_src.at[2, hi], rs_rcv.at[1, hi], rs_s.at[5], rs_r.at[5], down)
     from_z(bz_rcv, bz_r)
 
     pre = p_own[3]
-    landed(rs_rcv.at[0, hi], rs_r.at[2])
-    landed(rs_rcv.at[1, lo], rs_r.at[3])
-    landed(rs_rcv.at[0, lo], rs_r.at[4])
-    landed(rs_rcv.at[1, hi], rs_r.at[5])
-    pre = pre + rs_rcv[0].astype(F32) + rs_rcv[1].astype(F32)
+    for place in range(3):
+        landed(rs_rcv.at[place], rs_r.at[place])
+        pre = pre + rs_rcv[place].astype(F32)
     sigma = 1.0 / (1.0 + jnp.exp(-pre))
     d_hidden = bz_rcv[...].reshape(TGT, HS).astype(F32)
     ag[0] = (d_hidden * (sigma * (1.0 + pre * (1.0 - sigma)))).astype(BF)
-    send(ag.at[0, lo], ag.at[3, lo], ag_s.at[0], ag_r.at[0], up)
-    send(ag.at[0, hi], ag.at[1, hi], ag_s.at[1], ag_r.at[1], down)
-    send(ag.at[0, hi], ag.at[3, hi], ag_s.at[2], ag_r.at[2], up)
-    send(ag.at[0, lo], ag.at[1, lo], ag_s.at[3], ag_r.at[3], down)
+    send(ag.at[0], ag.at[3], ag_s.at[0], ag_r.at[0], up)
+    send(ag.at[0], ag.at[1], ag_s.at[1], ag_r.at[1], down)
+    send(ag.at[0], ag.at[2], ag_s.at[2], ag_r.at[2], across)
     fz_src[...] = (pre * sigma).astype(BF).reshape(Q, 32, HS)
     to_z(fz_src, fz_rcv, fz_s, fz_r)
 
@@ -409,18 +396,13 @@
     lower(0)
     scatter(0)
 
-    landed(ag.at[3, lo], ag_r.at[0])
-    send(ag.at[3, lo], ag.at[2, lo], ag_s.at[4], ag_r.at[4], up)
-    landed(ag.at[1, hi], ag_r.at[1])
-    send(ag.at[1, hi], ag.at[2, hi], ag_s.at[5], ag_r.at[5], down)
-
     from_z(ez_rcv, ez_r)
     collected = ez_rcv[...].reshape(TGT, 2 * CP).astype(F32).T.astype(BF)
     gup[...] = dot(collected, fz_src[...].reshape(TGT, HS)).astype(BF).reshape(Q, PIECE, HS)
     scatter_upper()
 
-    landed(ag.at[3, hi], ag_r.at[2])
-    landed(ag.at[1, lo], ag_r.at[3])
+    landed(ag.at[3], ag_r.at[0])
+    landed(ag.at[1], ag_r.at[1])
     grads = dot(xt[...].reshape(4 * FSL, TGT), jnp.concatenate([ag[3], ag[1]], axis=1)).astype(BF)
     gst[:, slots[3]] = grads[:, 0:HS].reshape(Q, PIECE, HS)
     gst[:, slots[1]] = grads[:, HS:2 * HS].reshape(Q, PIECE, HS)
@@ -430,8 +412,7 @@
     fw_src[...] = dot(perm[...], fz_rcv[...].reshape(TGT, HS)).astype(BF).reshape(Q, 32, HS)
     to_w(fw_src, fw_rcv, fw_s, fw_r)
 
-    landed(ag.at[2, lo], ag_r.at[4])
-    landed(ag.at[2, hi], ag_r.at[5])
+    landed(ag.at[2], ag_r.at[2])
     lower(2)
     scatter(2)
     scatter_z(0)
@@ -524,7 +505,7 @@
         vm((2, 2 * FSL, TGT), BF), vm((2, TGT, TGT), BF), vm((CP, TGT), BF), vm((2 * CP, HS), BF),
         vm((TGT, TGT), BF),
         vm((4, 2 * FSL, HS), BF), vm((4, TGT, HS), F32), vm((3, TGT, HS), BF),
-        vm((2, 128, HS), BF), vm((2, TGT, HS), BF),
+        vm((3, TGT, HS), BF),
         blocks, blocks, blocks, blocks, wide, wide, wide, wide,
         blocks, blocks, blocks, blocks,
         vm((4, TGT, HS), BF), vm((Q, 4, PIECE, HS), BF), vm((Q, PIECE, HS), BF),

time: 60.7 us -> 60.4 us (level)
  no operation moved by 1% of the time
where the time goes in v8:
time: 60.4 us; the launch traced here: 60.2 us
  Pallas kernels  59.6 us (99%)
  between operations  0.64 us (1%)
    pallas_call x1, Pallas kernels, local(): pl.pallas_call(main_kernel, out_shape=(jax.ShapeDtypeStruct((Q, 19, 16, H...  57.5 us
    pallas_call x1, Pallas kernels, local(): pl.pallas_call(finish_kernel, out_shape=(jax.ShapeDtypeStruct((C, TGT), F...  2.11 us

profile of v8, /device:TPU:1, one launch (start us, length us, event | category | flops | bytes accessed | tf_op | source)
XLA Modules:
  0.0 60.2 jit_solution(7652316281611507728)
XLA Ops:
  0.6 57.5 %sage_step.1 = (bf16[8,19,16,128]{3,2,1,0:T(8,128)(2,1)}, bf16[5,32,256]{2,1,0:T(8,128)(2,1)}) custom-call(bf16[96,1024]{1,0:T(8,128)(2,1)} %bitcast.11, s32[25,256]{1,0:T(8,128)} %bitcast.15, s32[1,256]{1,0:T(1,128)} %bitcast.17, s32[1,256]{1,0:T(1,128)} %bitcast.18, s32[15,256]{1,0:T(8,128)} %bitcast.16, bf16[96,1024]{1,0:T(8,128)(2,1)} %w1s_hbm.1, ...), custom_call_target="tpu_custom_call" | custom-call | tf_op jit(solution)/shard_map/sage_step/pallas_call | solution.py:521
  58.1 2.1 %finish.1 = (f32[153,256]{1,0:T(8,128)}, f32[96,1024]{1,0:T(8,128)}, f32[96,1024]{1,0:T(8,128)}, f32[153,128]{1,0:T(8,128)}, f32[153,128]{1,0:T(8,128)}) custom-call(bf16[8,19,16,128]{3,2,1,0:T(8,128)(2,1)} %get-tuple-element.12.gath, bf16[5,32,256]{2,1,0:T(8,128)(2,1)} %get-tuple-element.13.lout), custom_call_target="tpu_custom_call" | custom-call | tf_op jit(solution)/shard_map/finish/pallas_call | solution.py:538

commit v9 on v8

--- a/solution.py
+++ b/solution.py
@@ -412,10 +412,10 @@
     fw_src[...] = dot(perm[...], fz_rcv[...].reshape(TGT, HS)).astype(BF).reshape(Q, 32, HS)
     to_w(fw_src, fw_rcv, fw_s, fw_r)
 
+    scatter_z(0)
     landed(ag.at[2], ag_r.at[2])
     lower(2)
     scatter(2)
-    scatter_z(0)
     scatter_z(1)
 
     from_w(fw_rcv, fw_r)
@@ -431,8 +431,8 @@
 
     send_each(logit_part, lambda d: f_peer(d)[0] < LP)
 
+    gather_z(0)
     exchange_z()
-    gather_z(0)
     gather_z(1)
 
     fl = lax.rem(f, LP)

time: 60.4 us -> 60.2 us (level)
  no operation moved by 1% of the time
where the time goes in v9:
time: 60.2 us; the launch traced here: 60.1 us
  Pallas kernels  59.4 us (99%)
  between operations  0.64 us (1%)
    pallas_call x1, Pallas kernels, local(): pl.pallas_call(main_kernel, out_shape=(jax.ShapeDtypeStruct((Q, 19, 16, H...  57.3 us
    pallas_call x1, Pallas kernels, local(): pl.pallas_call(finish_kernel, out_shape=(jax.ShapeDtypeStruct((C, TGT), F...  2.11 us

profile of v9, /device:TPU:1, one launch (start us, length us, event | category | flops | bytes accessed | tf_op | source)
XLA Modules:
  0.0 60.1 jit_solution(16687487125864831958)
XLA Ops:
  0.6 57.3 %sage_step.1 = (bf16[8,19,16,128]{3,2,1,0:T(8,128)(2,1)}, bf16[5,32,256]{2,1,0:T(8,128)(2,1)}) custom-call(bf16[96,1024]{1,0:T(8,128)(2,1)} %bitcast.11, s32[25,256]{1,0:T(8,128)} %bitcast.15, s32[1,256]{1,0:T(1,128)} %bitcast.17, s32[1,256]{1,0:T(1,128)} %bitcast.18, s32[15,256]{1,0:T(8,128)} %bitcast.16, bf16[96,1024]{1,0:T(8,128)(2,1)} %w1s_hbm.1, ...), custom_call_target="tpu_custom_call" | custom-call | tf_op jit(solution)/shard_map/sage_step/pallas_call | solution.py:521
  57.9 2.1 %finish.1 = (f32[153,256]{1,0:T(8,128)}, f32[96,1024]{1,0:T(8,128)}, f32[96,1024]{1,0:T(8,128)}, f32[153,128]{1,0:T(8,128)}, f32[153,128]{1,0:T(8,128)}) custom-call(bf16[8,19,16,128]{3,2,1,0:T(8,128)(2,1)} %get-tuple-element.12.gath, bf16[5,32,256]{2,1,0:T(8,128)(2,1)} %get-tuple-element.13.lout), custom_call_target="tpu_custom_call" | custom-call | tf_op jit(solution)/shard_map/finish/pallas_call | solution.py:538

commit v10 on v4

--- a/solution.py
+++ b/solution.py
@@ -425,11 +425,11 @@
     fw_src[...] = dot(perm[...], fz_rcv[...].reshape(TGT, HS)).astype(BF).reshape(Q, 32, HS)
     to_w(fw_src, fw_rcv, fw_s, fw_r)
 
+    scatter_z(0)
     landed(ag.at[2, lo], ag_r.at[4])
     landed(ag.at[2, hi], ag_r.at[5])
     lower(2)
     scatter(2)
-    scatter_z(0)
     scatter_z(1)
 
     from_w(fw_rcv, fw_r)
@@ -445,8 +445,8 @@
 
     send_each(logit_part, lambda d: f_peer(d)[0] < LP)
 
+    gather_z(0)
     exchange_z()
-    gather_z(0)
     gather_z(1)
 
     fl = lax.rem(f, LP)

time: 60 us -> 59.6 us (level)
  no operation moved by 1% of the time
where the time goes in v10:
time: 59.6 us; the launch traced here: 59.5 us
  Pallas kernels  58.8 us (99%)
  between operations  0.64 us (1%)
    pallas_call x1, Pallas kernels, local(): pl.pallas_call(main_kernel, out_shape=(jax.ShapeDtypeStruct((Q, 19, 16, H...  56.7 us
    pallas_call x1, Pallas kernels, local(): pl.pallas_call(finish_kernel, out_shape=(jax.ShapeDtypeStruct((C, TGT), F...  2.11 us

profile of v10, /device:TPU:1, one launch (start us, length us, event | category | flops | bytes accessed | tf_op | source)
XLA Modules:
  0.0 59.5 jit_solution(7872404314044384613)
XLA Ops:
  0.6 56.7 %sage_step.1 = (bf16[8,19,16,128]{3,2,1,0:T(8,128)(2,1)}, bf16[5,32,256]{2,1,0:T(8,128)(2,1)}) custom-call(bf16[96,1024]{1,0:T(8,128)(2,1)} %bitcast.11, s32[25,256]{1,0:T(8,128)} %bitcast.15, s32[1,256]{1,0:T(1,128)} %bitcast.17, s32[1,256]{1,0:T(1,128)} %bitcast.18, s32[15,256]{1,0:T(8,128)} %bitcast.16, bf16[96,1024]{1,0:T(8,128)(2,1)} %w1s_hbm.1, ...), custom_call_target="tpu_custom_call" | custom-call | tf_op jit(solution)/shard_map/sage_step/pallas_call | solution.py:535
  57.4 2.1 %finish.1 = (f32[153,256]{1,0:T(8,128)}, f32[96,1024]{1,0:T(8,128)}, f32[96,1024]{1,0:T(8,128)}, f32[153,128]{1,0:T(8,128)}, f32[153,128]{1,0:T(8,128)}) custom-call(bf16[8,19,16,128]{3,2,1,0:T(8,128)(2,1)} %get-tuple-element.12.gath, bf16[5,32,256]{2,1,0:T(8,128)(2,1)} %get-tuple-element.13.lout), custom_call_target="tpu_custom_call" | custom-call | tf_op jit(solution)/shard_map/finish/pallas_call | solution.py:552
